TPU v7x, 128 devices: a whole 4x4x4 slice. The times are simulated.
128 devices in a mesh: clus: 8 (over y, core), pen: 16 (over x, z).
Axes of the slice: x: 4, y: 4, z: 4, core: 2. Of those that a mesh axis runs over, the one named last changes fastest.
Arguments:
- charges: bfloat16 [262144], P(('clus', 'pen')), may hold values from -6 to 6
- stencil: float32 [27, 262144], P(None, ('clus', 'pen')), may hold values from -3 to 3
- corner_cells: int32 [3, 262144], P(None, ('clus', 'pen')), may hold values from 0 to 253, as said below
- cluster_sizes: int32 [1024], P(('clus', 'pen')), may hold values from 1 to 256, as said below
- near_source: int32 [4096], P(('clus', 'pen')), may hold values from 0 to 1023, as said below
- near_blocks: bfloat16 [4096, 256, 256], P(('clus', 'pen')), may hold values from -0.1875 to 0.1875
- green_spectrum: float32 [512, 512, 512], P(None, 'clus', 'pen'), may hold values from 0.05 to 1
Outputs:
- potential: float32 [262144], P(('clus', 'pen'))
Inputs may be any that keep to these rules, and one draw needn't show every extreme that they name: `corner_cells`: each stencil box lies in the grid; along the first dimension it lies within the 256 / 8 planes of the clus index that holds the panel. `cluster_sizes`: every device holds a cluster of exactly 256 live panels. `near_source`: the first block of each cluster has the cluster itself as source; the other sources lie on the same or an adjacent clus index.
All inputs are finite; a program needn't handle non-finite values.
Results may differ from a plain program's by a relative error of at most 0.0006.
Values may be sent and summed in bfloat16 or wider, within the bound.
No kernel may reach another device: no remote copies, remote signals or barrier semaphores. Data moves between devices by JAX's collectives and lax.ppermute only.
A program may use at most 128 MiB of HBM per device.

v0:
```python
import functools
import math

import jax
import jax.numpy as jnp
import ml_dtypes
import numpy as np
from jax import lax
from jax.experimental import pallas as pl
from jax.experimental.pallas import tpu as pltpu
from jax.sharding import PartitionSpec as P

M = 256
L = 512
CAP = 256
NB = 4
SLOTS = 384
PENS = 16
DEVS = 128
ROOM = PENS * SLOTS + 512
TILE = 256
ROWS = 48
FIELDS = 24

exact = lax.Precision.HIGHEST
f32 = jnp.float32
bf16 = jnp.bfloat16
NT = (((1,), (1,)), ((), ()))


def section_table(count, length, sign):
    sample = jnp.arange(count, dtype=jnp.int32)[:, None]
    wave_number = jnp.arange(length, dtype=jnp.int32)[None, :]
    phase = (sample * wave_number % length).astype(jnp.float32) * (2.0 * math.pi / length)
    cosine = jnp.cos(phase)
    sine = jnp.sin(phase)
    from_real = jnp.stack([cosine, sign * sine], axis=1)
    from_imag = jnp.stack([-sign * sine, cosine], axis=1)
    return jnp.stack([from_real, from_imag], axis=0)


def exchanged(x, axis, split):
    return lax.all_to_all(x.astype(bf16), axis, split_axis=split, concat_axis=split + 1, tiled=True)


def far_field_general(charge_value, stencil, corner_cells, green_spectrum):
    pen_count = lax.axis_size("pen")
    clus_count = lax.axis_size("clus")
    planes = M // clus_count
    rows_own = M // pen_count
    pen_spread = L // pen_count
    clus_spread = L // clus_count
    slab_index = lax.axis_index("clus")
    forward_table = section_table(M, L, -1.0)
    inverse_table = section_table(M, L, 1.0)
    offset = jnp.arange(27, dtype=jnp.int32)[:, None]
    first = corner_cells[0][None, :] + offset // 9 - slab_index * planes
    second = corner_cells[1][None, :] + offset // 3 % 3
    third = corner_cells[2][None, :] + offset % 3
    slab_cell = (first * M + second) * M + third
    deposit = stencil * charge_value[None, :]
    slab_charge = (
        jnp.zeros((planes * M * M,), f32).at[slab_cell.reshape(-1)].add(deposit.reshape(-1))
    )
    grid_block = lax.psum_scatter(
        slab_charge.reshape(planes, M, M), "pen", scatter_dimension=1, tiled=True
    )
    section = jnp.einsum("xyz,zdk->dxyk", grid_block, forward_table[0], precision=exact)
    section = (
        section.reshape(2, planes, rows_own, pen_count, pen_spread)
        .transpose(0, 3, 2, 1, 4)
        .reshape(2, pen_count, rows_own, planes * pen_spread)
    )
    section = exchanged(section, "pen", 1).reshape(2, M, planes * pen_spread).astype(f32)
    section = jnp.einsum("cyw,cydk->dkw", section, forward_table, precision=exact)
    section = (
        section.reshape(2, clus_count, clus_spread, planes, pen_spread)
        .transpose(0, 1, 3, 2, 4)
        .reshape(2, clus_count, planes, clus_spread * pen_spread)
    )
    section = exchanged(section, "clus", 1).reshape(2, M, clus_spread * pen_spread).astype(f32)
    spectrum = jnp.einsum("cxv,cxdk->dkv", section, forward_table, precision=exact)
    spectrum = spectrum * green_spectrum.reshape(1, L, clus_spread * pen_spread)
    section = jnp.einsum("ckv,cxdk->dxv", spectrum, inverse_table, precision=exact)
    section = (
        section.reshape(2, clus_count, planes, clus_spread, pen_spread)
        .transpose(0, 1, 3, 2, 4)
        .reshape(2, clus_count, clus_spread, planes * pen_spread)
    )
    section = exchanged(section, "clus", 1).reshape(2, L, planes * pen_spread).astype(f32)
    section = jnp.einsum("ckw,cydk->dyw", section, inverse_table, precision=exact)
    section = (
        section.reshape(2, pen_count, rows_own, planes, pen_spread)
        .transpose(0, 1, 4, 2, 3)
        .reshape(2, pen_count, pen_spread, rows_own * planes)
    )
    section = exchanged(section, "pen", 1).reshape(2, L, rows_own * planes).astype(f32)
    lines = jnp.einsum("ckw,czk->zw", section, inverse_table[:, :, 0, :], precision=exact)
    lines = lines * (1.0 / (L * L * L))
    block = lines.reshape(M, rows_own, planes).transpose(2, 1, 0)
    slab = lax.all_gather(block, "pen", axis=1, tiled=True)
    return jnp.sum(stencil * slab.reshape(-1)[slab_cell], axis=0)


def rounded(x):
    return x.astype(np.float32).astype(ml_dtypes.bfloat16).astype(np.float64)


def balanced(exact_values):
    near = rounded(exact_values)
    ulp = np.ldexp(1.0, np.frexp(exact_values)[1] - 8)
    error = near - exact_values
    other = near - np.sign(error) * ulp
    gain = (other - near) * exact_values
    cost = (other - exact_values) ** 2 - error**2
    for x in range(exact_values.shape[1]):
        bias = np.sum(error[:, x] * exact_values[:, x])
        order = np.argsort(cost[:, x] / np.maximum(np.abs(gain[:, x]), 1e-30))
        for i in order:
            if error[i, x] != 0.0 and np.abs(bias + gain[i, x]) < np.abs(bias):
                near[i, x] = other[i, x]
                bias += gain[i, x]
            if np.abs(bias) < 1e-4:
                break
    return near


@functools.cache
def tables():
    plane = np.concatenate([2 * np.arange(DEVS), 2 * np.arange(DEVS) + 1])
    own = np.arange(L).reshape(PENS, 8, 4).transpose(1, 0, 2).reshape(-1)
    phase = (np.outer(np.arange(L), np.arange(M)) % L) * (2.0 * np.pi / L)
    both = balanced(np.concatenate([np.cos(phase), np.sin(phase)], axis=0))
    cos, sin = both[:L], both[L:]
    along_z = np.stack([cos[own], -sin[own]], axis=1).reshape(2 * L, M)
    back_z = along_z.T / float(L) ** 3
    along_y = np.block([[cos, sin], [-sin, cos]])
    back_y = along_y.T
    cos, sin = cos.T[plane], sin.T[plane]
    along_x = np.block([[cos, -sin], [sin, cos]])
    back_x = along_x
    return tuple(
        t.astype(np.float32).astype(ml_dtypes.bfloat16)
        for t in (along_z, along_y, along_x, back_y, back_x, back_z)
    )


def iota(shape, dim):
    return lax.broadcasted_iota(jnp.int32, shape, dim)


def bucket_kernel(
    slab_ref, sizes_ref, charge_ref, stencil_ref, corner_ref, out_ref, route_ref,
    first_ref, second_ref, total_ref,
):
    count = 8 * CAP
    lane = iota((1, CAP), 1)
    charge = charge_ref[...].astype(f32)
    live = jnp.concatenate(
        [jnp.where(lane < sizes_ref[k], 1.0, 0.0) for k in range(8)], axis=1
    )
    row8 = iota((8, CAP), 0)
    size8 = jnp.zeros((8, CAP), jnp.int32)
    for k in range(8):
        size8 = jnp.where(row8 == k, sizes_ref[k], size8)
    charge = jnp.where(iota((8, CAP), 1) < size8, charge, 0.0)
    q = jnp.concatenate([charge[k : k + 1] for k in range(8)], axis=1)
    x = corner_ref[0:1, :] - slab_ref[0] * 32
    owner = jnp.where(live > 0.0, x >> 1, -2)
    odd = (x & 1) == 1
    pen = iota((PENS, count), 0)
    member = jnp.where((pen == owner) | (pen == owner + 1), 1.0, 0.0)
    upper = jnp.where(iota((128, 128), 0) <= iota((128, 128), 1), 1.0, 0.0).astype(bf16)
    carry = jnp.zeros((PENS, 128), f32)
    ranks = []
    for k in range(count // 128):
        part = member[:, 128 * k : 128 * k + 128]
        upto = jnp.dot(part.astype(bf16), upper, preferred_element_type=f32) + carry
        ranks.append(upto - part)
        carry = jnp.broadcast_to(upto[:, 127:128], (PENS, 128))
    rank = jnp.concatenate(ranks, axis=1)
    over = jnp.where(jnp.max(carry, axis=0, keepdims=True) > SLOTS, 1.0, 0.0)
    over = jnp.concatenate([over] * (SLOTS // 128), axis=1)
    pos_first = jnp.sum(jnp.where(pen == owner, rank, 0.0), axis=0, keepdims=True)
    pos_second = jnp.sum(jnp.where(pen == owner + 1, rank, 0.0), axis=0, keepdims=True)
    pos_first = jnp.where(live > 0.0, pos_first, -1.0).astype(jnp.int32)
    pos_second = jnp.where(live > 0.0, pos_second, -1.0).astype(jnp.int32)
    route_ref[...] = jnp.zeros((8, count), jnp.int32)
    route_ref[0:1, :] = owner
    route_ref[1:2, :] = pos_first
    route_ref[2:3, :] = pos_second

    for ref in (first_ref, second_ref):
        ref[...] = jnp.zeros((ROWS, count), f32)
        ref[18:19, :] = q
        ref[19:20, :] = corner_ref[1:2, :].astype(f32)
        ref[20:21, :] = corner_ref[2:3, :].astype(f32)
        ref[21:22, :] = live
    w0 = stencil_ref[0:9, :]
    w1 = stencil_ref[9:18, :]
    w2 = stencil_ref[18:27, :]
    first_ref[0:9, :] = jnp.where(odd, 0.0, w0)
    first_ref[9:18, :] = jnp.where(odd, w0, w1)
    second_ref[0:9, :] = jnp.where(odd, w1, w2)
    second_ref[9:18, :] = jnp.where(odd, w2, 0.0)
    for ref in (first_ref, second_ref):
        w = ref[0:18, :]
        ref[24:42, :] = w - w.astype(bf16).astype(f32)

    step = 512
    total_ref[...] = jnp.zeros_like(total_ref)

    def chunk(k, _):
        at = pl.ds(pl.multiple_of(k * step, step), step)
        own = route_ref[0:1, at]
        slot = iota((SLOTS, step), 0)
        for ref, shift, row in ((first_ref, 0, 1), (second_ref, 1, 2)):
            values = ref[:, at].astype(bf16)
            spread = jnp.concatenate(
                [
                    values * jnp.where(own + shift == p, 1.0, 0.0).astype(bf16)
                    for p in range(PENS)
                ],
                axis=0,
            )
            hot = jnp.where(slot == route_ref[row : row + 1, at], 1.0, 0.0).astype(bf16)
            total_ref[...] += lax.dot_general(spread, hot, NT, preferred_element_type=f32)
        return 0

    lax.fori_loop(0, count // step, chunk, 0)
    first_ref[...] = jnp.zeros_like(first_ref)
    first_ref[22:23, 0:SLOTS] = over
    first_ref[42:48, 0:CAP] = charge[0:6]
    for k in range(4):
        half = slice(k % 2 * 128, k % 2 * 128 + 128)
        first_ref[42 + k : 43 + k, CAP:SLOTS] = charge[6 + k // 2 : 7 + k // 2, half]
    extra = first_ref[:, 0:SLOTS]
    for p in range(PENS):
        out_ref[p] = (total_ref[ROWS * p : ROWS * p + ROWS, :] + extra).astype(bf16)


def hot_z(z, c):
    return jnp.where(iota((M, TILE), 0) == z + c, 1.0, 0.0).astype(bf16)


def deposit_kernel(
    recv_ref, table_ref, out_ref, packed_ref, meta_ref, left_ref, right_ref,
    low_ref, grid_ref,
):
    packed_ref[...] = jnp.zeros_like(packed_ref)
    blocks = [recv_ref[s].astype(f32) for s in range(PENS)]
    counts = [jnp.sum(b[21:22, :]).astype(jnp.int32) for b in blocks]
    start = jnp.int32(0)
    for s in range(PENS):
        meta_ref[s] = start
        block = blocks[s][:FIELDS] + jnp.concatenate(
            [blocks[s][FIELDS : FIELDS + 18], jnp.zeros((FIELDS - 18, SLOTS), f32)], axis=0
        )
        block = jnp.concatenate([block, jnp.zeros((FIELDS, 128), f32)], axis=1)
        block = pltpu.roll(block, start % 128, 1)
        at = pl.ds(pl.multiple_of(start // 128 * 128, 128), SLOTS + 128)
        packed_ref[:, at] = packed_ref[:, at] + block
        start = start + counts[s]
    meta_ref[PENS] = start
    over = blocks[0][22:23, :128]
    for s in range(1, PENS):
        over = jnp.maximum(over, blocks[s][22:23, :128])
    spoil = jnp.where(over[:, :1] > 0.0, jnp.nan, 0.0)
    grid_ref[...] = jnp.zeros_like(grid_ref)

    def tile(r, _):
        fields = packed_ref[:, pl.ds(pl.multiple_of(r * TILE, TILE), TILE)]
        y = fields[19:20].astype(jnp.int32)
        z = fields[20:21].astype(jnp.int32)
        weights = fields[0:18] * fields[18:19]
        away = iota((M, TILE), 0) - y
        is0, is1, is2 = away == 0, away == 1, away == 2
        for c in range(3):
            left_ref[:, c * TILE : (c + 1) * TILE] = hot_z(z, c)
            for xp in range(2):
                w = [weights[xp * 9 + b * 3 + c : xp * 9 + b * 3 + c + 1] for b in range(3)]
                v = jnp.where(is0, w[0], jnp.where(is1, w[1], jnp.where(is2, w[2], 0.0)))
                high = v.astype(bf16)
                low = (v - high.astype(f32)).astype(bf16)
                right_ref[xp * M : (xp + 1) * M, c * TILE : (c + 1) * TILE] = high
                low_ref[xp * M : (xp + 1) * M, c * TILE : (c + 1) * TILE] = low
        left = left_ref[...]
        grid_ref[...] += lax.dot_general(
            left, right_ref[...], NT, preferred_element_type=f32
        ) + lax.dot_general(left, low_ref[...], NT, preferred_element_type=f32)
        return 0

    lax.fori_loop(0, (start + TILE - 1) // TILE, tile, 0)
    grid = grid_ref[...] + spoil
    high = grid.astype(bf16)
    low = (grid - high.astype(f32)).astype(bf16)
    for k in range(4):
        at = slice(k * 256, k * 256 + 256)
        table = table_ref[at, :]
        out_ref[at, :] = (
            jnp.dot(table, high, preferred_element_type=f32)
            + jnp.dot(table, low, preferred_element_type=f32)
        ).astype(bf16)


def convolve_kernel(
    recv_ref, green_ref, along_y_ref, along_x_ref, back_y_ref, back_x_ref, out_ref, in_ref, sum_ref
):
    j = pl.program_id(0)

    @pl.when(j == 0)
    def _():
        for h in range(4):
            in_ref[h] = recv_ref[:, h * 128 : h * 128 + 128].astype(f32)

    def piece(xp):
        return jnp.concatenate(
            [
                in_ref[2 * xp + h, pl.ds(2 * j + c, DEVS, stride=8), :].astype(bf16)
                for c in range(2)
                for h in range(2)
            ],
            axis=1,
        )

    field = jnp.concatenate([piece(0), piece(1)], axis=0)
    part = lax.dot_general(along_y_ref[...], field, NT, preferred_element_type=f32).astype(bf16)
    part = jnp.concatenate([part[:L], part[L:]], axis=1)
    part = jnp.dot(part, along_x_ref[...], preferred_element_type=f32)
    green = green_ref[...].reshape(L, L).astype(f32)
    part = jnp.concatenate(
        [(part[:, :L] * green).astype(bf16), (part[:, L:] * green).astype(bf16)], axis=0
    )
    part = jnp.dot(back_y_ref[...], part, preferred_element_type=f32).astype(bf16)
    part = jnp.concatenate([part[:M], part[M:]], axis=1)
    part = lax.dot_general(back_x_ref[...], part, NT, preferred_element_type=f32)
    for c in range(2):
        for xp in range(2):
            row = c * M + xp * DEVS
            for h in range(2):
                sum_ref[2 * xp + h, pl.ds(2 * j + c, DEVS, stride=8), :] = part[
                    row : row + DEVS, h * 128 : h * 128 + 128
                ]

    @pl.when(j == 3)
    def _():
        for h in range(4):
            out_ref[:, h * 128 : h * 128 + 128] = sum_ref[h].astype(bf16)


def interpolate_kernel(meta_ref, recv_ref, table_ref, packed_ref, out_ref, flag_ref, grid_ref, result_ref):
    grid = jnp.dot(table_ref[...], recv_ref[...], preferred_element_type=f32)
    flag_ref[...] = jnp.where(jnp.isnan(grid[:8, :128]), 1.0, 0.0)
    grid = grid.T
    high = grid.astype(bf16)
    grid_ref[0] = high
    grid_ref[1] = (grid - high.astype(f32)).astype(bf16)
    result_ref[...] = jnp.zeros_like(result_ref)

    def tile(r, _):
        at = pl.ds(pl.multiple_of(r * TILE, TILE), TILE)
        fields = packed_ref[:, at]
        y = fields[19:20].astype(jnp.int32)
        z = fields[20:21].astype(jnp.int32)
        away = iota((M, TILE), 0) - y
        is0, is1, is2 = away == 0, away == 1, away == 2
        total = jnp.zeros((M, TILE), f32)
        for c in range(3):
            hot = hot_z(z, c)
            near = jnp.dot(grid_ref[0], hot, preferred_element_type=f32) + jnp.dot(
                grid_ref[1], hot, preferred_element_type=f32
            )
            for xp in range(2):
                w = [fields[xp * 9 + b * 3 + c : xp * 9 + b * 3 + c + 1] for b in range(3)]
                v = jnp.where(is0, w[0], jnp.where(is1, w[1], jnp.where(is2, w[2], 0.0)))
                total = total + v * near[xp * M : (xp + 1) * M]
        result_ref[:, at] = jnp.broadcast_to(jnp.sum(total, axis=0, keepdims=True), (8, TILE))
        return 0

    lax.fori_loop(0, (meta_ref[PENS] + TILE - 1) // TILE, tile, 0)
    width = SLOTS + 128
    for s in range(PENS):
        start = meta_ref[s]
        piece = result_ref[:, pl.ds(pl.multiple_of(start // 128 * 128, 128), width)]
        piece = pltpu.roll(piece, (width - start % 128) % width, 1)
        out_ref[s : s + 1, :] = piece[0:1, :SLOTS]


def collect_kernel(back_ref, route_ref, out_ref):
    back = back_ref[...]
    high = back.astype(bf16)
    low = (back - high.astype(f32)).astype(bf16)
    both = jnp.concatenate([high.astype(f32), low.astype(f32)], axis=0).astype(bf16)
    step = 512
    for k in range(4):
        at = slice(k * step, k * step + step)
        owner = route_ref[0:1, at]
        slot = iota((SLOTS, step), 0)
        pen = iota((PENS, step), 0)
        total = jnp.zeros((PENS, step), f32)
        for shift in range(2):
            hot = jnp.where(slot == route_ref[shift + 1 : shift + 2, at], 1.0, 0.0).astype(bf16)
            got = jnp.dot(both, hot, preferred_element_type=f32)
            total = total + jnp.where(pen == owner + shift, got[:PENS] + got[PENS:], 0.0)
        out_ref[:, at] = jnp.broadcast_to(jnp.sum(total, axis=0, keepdims=True), (8, step))


def struct(shape, dtype):
    return jax.ShapeDtypeStruct(shape, dtype)


def whole(count):
    return [pl.BlockSpec(memory_space=pltpu.VMEM)] * count


SMEM = pl.BlockSpec(memory_space=pltpu.SMEM)
LIMIT = pltpu.CompilerParams(vmem_limit_bytes=40 * 1024 * 1024)


def far_field_blocks(charges, stencil, corner_cells, cluster_sizes, green_spectrum):
    along_z, along_y, along_x, back_y, back_x, back_z = [jnp.asarray(t) for t in tables()]
    green = (
        green_spectrum.astype(bf16).transpose(2, 1, 0).reshape(8, 4, L // 8, L)
    )
    green = lax.all_to_all(green, "clus", 0, 0, tiled=True)
    sent, route = pl.pallas_call(
        bucket_kernel,
        out_shape=[
            struct((PENS, ROWS, SLOTS), bf16),
            struct((8, 8 * CAP), jnp.int32),
        ],
        in_specs=[SMEM, SMEM] + whole(3),
        out_specs=whole(2),
        scratch_shapes=[
            pltpu.VMEM((ROWS, 8 * CAP), f32),
            pltpu.VMEM((ROWS, 8 * CAP), f32),
            pltpu.VMEM((ROWS * PENS, SLOTS), f32),
        ],
        compiler_params=LIMIT,
        name="bucket",
    )(
        lax.axis_index("clus").astype(jnp.int32).reshape(1),
        cluster_sizes,
        charges.reshape(8, CAP),
        stencil,
        corner_cells,
    )
    recv = lax.all_to_all(sent, "pen", 0, 0, tiled=True)
    section, packed, meta = pl.pallas_call(
        deposit_kernel,
        out_shape=[
            struct((2 * L, 2 * M), bf16),
            struct((FIELDS, ROOM), f32),
            struct((PENS + 1,), jnp.int32),
        ],
        in_specs=whole(2),
        out_specs=whole(2) + [SMEM],
        scratch_shapes=[
            pltpu.VMEM((M, 3 * TILE), bf16),
            pltpu.VMEM((2 * M, 3 * TILE), bf16),
            pltpu.VMEM((2 * M, 3 * TILE), bf16),
            pltpu.VMEM((M, 2 * M), f32),
        ],
        compiler_params=LIMIT,
        name="deposit",
    )(recv, along_z)
    section, green = lax.optimization_barrier((section, green))
    section = lax.all_to_all(
        section.reshape(DEVS, 8, 2 * M), ("clus", "pen"), 0, 0, tiled=True
    )
    section = pl.pallas_call(
        convolve_kernel,
        grid=(4,),
        out_shape=struct((2 * L, 2 * M), bf16),
        in_specs=[
            pl.BlockSpec((2 * L, 2 * M), lambda j: (0, 0)),
            pl.BlockSpec((8, 1, L // 8, L), lambda j: (0, j, 0, 0)),
            pl.BlockSpec((2 * L, 2 * M), lambda j: (0, 0)),
            pl.BlockSpec((2 * M, 2 * L), lambda j: (0, 0)),
            pl.BlockSpec((2 * M, 2 * L), lambda j: (0, 0)),
            pl.BlockSpec((2 * M, 2 * L), lambda j: (0, 0)),
        ],
        out_specs=pl.BlockSpec((2 * L, 2 * M), lambda j: (0, 0)),
        scratch_shapes=[
            pltpu.VMEM((4, 2 * L, 128), f32),
            pltpu.VMEM((4, 2 * L, 128), f32),
        ],
        compiler_params=LIMIT,
        name="convolve",
    )(section.reshape(2 * L, 2 * M), green, along_y, along_x, back_y, back_x)
    section = lax.all_to_all(
        section.reshape(DEVS, 8, 2 * M), ("clus", "pen"), 0, 0, tiled=True
    )
    back, flag = pl.pallas_call(
        interpolate_kernel,
        out_shape=[struct((PENS, SLOTS), f32), struct((8, 128), f32)],
        in_specs=[SMEM] + whole(3),
        out_specs=whole(2),
        scratch_shapes=[pltpu.VMEM((2, 2 * M, M), bf16), pltpu.VMEM((8, ROOM), f32)],
        compiler_params=LIMIT,
        name="interpolate",
    )(meta, section.reshape(2 * L, 2 * M), back_z, packed)
    back = lax.all_to_all(back, "pen", 0, 0, tiled=True)
    far = pl.pallas_call(
        collect_kernel,
        out_shape=struct((8, 8 * CAP), f32),
        in_specs=whole(2),
        out_specs=pl.BlockSpec(memory_space=pltpu.VMEM),
        compiler_params=LIMIT,
        name="collect",
    )(back, route)
    pool = jnp.concatenate(
        [recv[:, 42:48, :CAP], recv[:, 42:46, CAP:].reshape(PENS, 2, CAP)], axis=1
    ).reshape(PENS * 8, CAP)
    return far[0], pool, flag[0, 0]


def neighbours(x, axis):
    devices = lax.axis_size(axis)
    up = [(i, i + 1) for i in range(devices - 1)]
    before = lax.ppermute(x, axis, up)
    after = lax.ppermute(x, axis, [(j, i) for i, j in up])
    return jnp.concatenate([before, x, after], axis=0)


def per_device(
    charges, stencil, corner_cells, cluster_sizes, near_source, near_blocks, green_spectrum
):
    slot_rank = jnp.arange(CAP, dtype=jnp.int32)
    slot_mask = (slot_rank[None, :] < cluster_sizes[:, None]).reshape(-1)
    far_field, pool, overflow = far_field_blocks(
        charges, stencil, corner_cells, cluster_sizes, green_spectrum
    )
    local_source = near_source - (lax.axis_index("clus") - 1) * pool.shape[0]
    source_rows = neighbours(pool, "clus")[local_source]
    near_terms = jnp.einsum(
        "pjm,pm->pj", near_blocks, source_rows, preferred_element_type=f32
    )
    near_field = near_terms.reshape(-1, NB, CAP).sum(axis=1).reshape(-1)

    def general():
        charge_value = jnp.where(slot_mask, charges, jnp.zeros_like(charges)).astype(f32)
        return far_field_general(charge_value, stencil, corner_cells, green_spectrum)

    far_field = lax.cond(overflow > 0.0, general, lambda: far_field)
    total = far_field + near_field
    return jnp.where(slot_mask, total, jnp.zeros_like(total))


def solution(mesh):
    in_specs = (
        P(("clus", "pen")),
        P(None, ("clus", "pen")),
        P(None, ("clus", "pen")),
        P(("clus", "pen")),
        P(("clus", "pen")),
        P(("clus", "pen"), None, None),
        P(None, "clus", "pen"),
    )
    out_specs = P(("clus", "pen"))
    return jax.shard_map(
        per_device, mesh=mesh, in_specs=in_specs, out_specs=out_specs, check_vma=False
    )
```

profile of v0, /device:TPU:0, one launch (start us, length us, event | category | flops | bytes accessed | tf_op | source)
XLA Modules:
  0.0 154.5 jit_solution(236988188815264371)
XLA Ops:
  6.5 0.7 reshape.515.charge_ref
  7.2 0.0 copy-start.10
  7.2 0.7 copy-done.10
  7.9 7.2 %bucket.1 = (bf16[16,48,384]{2,1,0:T(8,128)(2,1)}, s32[8,2048]{1,0:T(8,128)S(1)}) custom-call(s32[1]{0:T(128)} %bitcast.47.slab_ref, s32[8]{0:T(128)S(1)} %copy-done.10, bf16[8,256]{1,0:T(8,128)(2,1)S(1)} %reshape.515.charge_ref, f32[27,2048]{1,0:T(8,128)} %stencil_ref.1, s32[3,2048]{1,0:T(4,128)} %corner_ref.1), custom_call_target="tpu_custom_call" | custom-call | tf_op jit(solution)/shard_map/bucket/pallas_call | solution.py:426
  15.1 8.0 %all-to-all-start.4 = ((bf16[16,48,384]{2,1,0:T(8,128)(2,1)}), bf16[16,48,384]{2,1,0:T(8,128)(2,1)S(1)}, u32[]{:S(2)}, u32[]{:S(2)}) async-start(bf16[16,48,384]{2,1,0:T(8,128)(2,1)} %get-tuple-element.36), calls=%async_computation.5 | async-start | bytes 1179648 | tf_op jit(solution)/shard_map/all_to_all | solution.py:448
  23.1 2.5 %convert_bitcast_fusion = bf16[32,64,512]{2,0,1:T(8,128)(2,1)S(1)} fusion(f32[512,64,32]{0,2,1:T(8,128)} %param.21), kind=kLoop, calls=%fused_computation.75 | loop fusion | flops 1048576 | bytes 6291456 | tf_op jit(solution)/shard_map/transpose | solution.py:423
  25.6 2.5 %copy.121 = bf16[32,64,512]{2,1,0:T(8,128)(2,1)} copy(bf16[32,64,512]{2,0,1:T(8,128)(2,1)S(1)} %convert_bitcast_fusion) | data formatting | bytes 4194304 | tf_op jit(solution)/shard_map/transpose | solution.py:423
  28.1 6.9 %all-to-all-done.4.recv_ref = bf16[16,48,384]{2,1,0:T(8,128)(2,1)S(1)} async-done(((bf16[16,48,384]{2,1,0:T(8,128)(2,1)}), bf16[16,48,384]{2,1,0:T(8,128)(2,1)S(1)}, u32[]{:S(2)}, u32[]{:S(2)}) %all-to-all-start.4) | async-done | bytes 589856 | tf_op jit(solution)/shard_map/all_to_all | solution.py:448
  35.0 0.0 copy-start.1
  35.0 0.8 copy-done.1
  35.8 4.5 %all-to-all-start.5 = ((bf16[8,4,64,512]{3,2,1,0:T(8,128)(2,1)}), bf16[8,4,64,512]{3,2,1,0:T(8,128)(2,1)S(1)}, u32[]{:S(2)}, u32[]{:S(2)}) async-start(bf16[8,4,64,512]{3,2,1,0:T(8,128)(2,1)} %bitcast.157), calls=%async_computation.6 | async-start | bytes 4194304 | tf_op jit(solution)/shard_map/all_to_all | solution.py:425
  40.3 0.0 copy-start.2
  40.3 1.1 copy-done.2
  41.3 0.0 copy-start.9
  41.3 1.0 copy-done.9
  42.4 0.0 copy-start
  42.4 4.9 %deposit.1 = (bf16[1024,512]{1,0:T(8,128)(2,1)S(1)}, f32[24,6656]{1,0:T(8,128)S(1)}, s32[17]{0:T(128)S(1)}) custom-call(bf16[16,48,384]{2,1,0:T(8,128)(2,1)S(1)} %copy-done.2, bf16[1024,256]{1,0:T(8,128)(2,1)S(1)} %copy-done.9), custom_call_target="tpu_custom_call" | custom-call | tf_op jit(solution)/shard_map/deposit/pallas_call | solution.py:449
  47.3 0.0 copy-start.3
  47.3 1.0 copy-done.3
  48.3 0.0 copy-start.6
  48.3 0.8 copy-done.6
  49.1 18.4 %all-to-all-done.5.green_ref = bf16[8,4,64,512]{3,2,1,0:T(8,128)(2,1)S(1)} async-done(((bf16[8,4,64,512]{3,2,1,0:T(8,128)(2,1)}), bf16[8,4,64,512]{3,2,1,0:T(8,128)(2,1)S(1)}, u32[]{:S(2)}, u32[]{:S(2)}) %all-to-all-start.5) | async-done | bytes 2097184 | tf_op jit(solution)/shard_map/all_to_all | solution.py:425
  67.5 0.0 copy-start.4
  67.5 0.0 copy-start.5
  67.5 24.0 %all_to_all.65 = bf16[128,8,512]{2,1,0:T(8,128)(2,1)S(1)} all-to-all(bf16[128,8,512]{2,1,0:T(8,128)(2,1)} %bitcast.147), channel_id=1, replica_groups=mesh['clus'=8,'pen'=16] {'clus','pen'}, dimensions={0} | all-to-all | bytes 2097152 | tf_op jit(solution)/shard_map/all_to_all | solution.py:468
  91.5 0.0 copy-done
  91.5 0.0 copy-done.4
  91.5 0.0 copy-done.5
  91.5 11.3 %convolve.1 = bf16[1024,512]{1,0:T(8,128)(2,1)} custom-call(bf16[1024,512]{1,0:T(8,128)(2,1)S(1)} %bitcast.146, bf16[8,4,64,512]{3,2,1,0:T(8,128)(2,1)S(1)} %all-to-all-done.5.green_ref, bf16[1024,512]{1,0:T(8,128)(2,1)S(1)} %copy-done.4, bf16[512,1024]{1,0:T(8,128)(2,1)S(1)} %copy-done, bf16[512,1024]{1,0:T(8,128)(2,1)S(1)} %copy-done.5, ...), custom_call_target="tpu_custom_call" | custom-call | tf_op jit(solution)/shard_map/convolve/pallas_call | solution.py:471
  102.8 0.0 copy-start.11
  102.8 0.0 copy-start.22
  102.8 4.8 %all-to-all-start.7 = ((bf16[128,8,512]{2,1,0:T(8,128)(2,1)}), bf16[128,8,512]{2,1,0:T(8,128)(2,1)S(1)}, u32[]{:S(2)}, u32[]{:S(2)}) async-start(bf16[128,8,512]{2,1,0:T(8,128)(2,1)} %bitcast.52), calls=%async_computation.8 | async-start | bytes 2097152 | tf_op jit(solution)/shard_map/all_to_all | solution.py:491
  107.6 0.0 copy-done.11
  107.6 0.1 iota_compare_fusion
  107.7 0.0 copy-done.22
  107.7 0.8 slice.33
  108.5 0.9 slice.32
  109.4 1.3 collective-permute-start
  110.7 1.3 collective-permute-start.1
  112.0 0.0 collective-permute-done
  112.1 2.9 %collective-permute-done.1 = bf16[128,256]{1,0:T(8,128)(2,1)S(1)} collective-permute-done((bf16[128,256]{1,0:T(8,128)(2,1)S(1)}, bf16[128,256]{1,0:T(8,128)(2,1)S(1)}, u32[]{:S(2)}, u32[]{:S(2)}) %collective-permute-start.1) | collective-permute-done | bytes 65568 | tf_op jit(solution)/shard_map/ppermute | solution.py:522
  115.0 0.6 gather_fusion.1
  115.6 11.0 %all-to-all-done.7 = bf16[128,8,512]{2,1,0:T(8,128)(2,1)S(1)} async-done(((bf16[128,8,512]{2,1,0:T(8,128)(2,1)}), bf16[128,8,512]{2,1,0:T(8,128)(2,1)S(1)}, u32[]{:S(2)}, u32[]{:S(2)}) %all-to-all-start.7) | async-done | bytes 1048608 | tf_op jit(solution)/shard_map/all_to_all | solution.py:491
  126.6 0.0 copy-done.7
  126.6 0.0 copy-done.8
  126.6 4.2 %interpolate.1 = (f32[16,384]{1,0:T(8,128)S(1)}, f32[8,128]{1,0:T(8,128)S(1)}) custom-call(s32[17]{0:T(128)S(1)} %get-tuple-element.37.meta_ref, bf16[1024,512]{1,0:T(8,128)(2,1)S(1)} %bitcast.145, bf16[256,1024]{1,0:T(8,128)(2,1)S(1)} %copy-done.8, f32[24,6656]{1,0:T(8,128)S(1)} %copy-done.7), custom_call_target="tpu_custom_call" | custom-call | tf_op jit(solution)/shard_map/interpolate/pallas_call | solution.py:494
  130.9 0.6 copy.122
  131.5 5.9 %all-to-all-start.8 = ((f32[16,1,384]{2,1,0:T(1,128)}), f32[16,1,384]{2,1,0:T(1,128)S(1)}, u32[]{:S(2)}, u32[]{:S(2)}) async-start(f32[16,1,384]{2,1,0:T(1,128)} %copy.122), calls=%async_computation.9 | async-start | bytes 49152 | tf_op jit(solution)/shard_map/all_to_all | solution.py:503
  137.4 0.0 copy-start.17
  137.4 0.0 copy-start.18
  137.5 0.0 copy-start.21
  137.5 3.4 %fusion.42 = f32[32,1,256]{2,1,0:T(1,128)S(1)} fusion(bf16[32,256,256]{2,1,0:T(8,128)(2,1)} %param.20, bf16[32,256,1]{1,0,2:T(8,128)(2,1)S(1)} %bitcast.167), kind=kOutput, calls=%fused_computation.79 | convolution fusion | flops 4194304 | bytes 4243456 | tf_op jit(solution)/shard_map/pjm,pm->pj/dot_general | solution.py:536
  140.9 0.6 copy.145
  141.6 0.5 slice.25
  142.7 2.4 %all-to-all-done.8 = f32[16,1,384]{2,1,0:T(1,128)S(1)} async-done(((f32[16,1,384]{2,1,0:T(1,128)}), f32[16,1,384]{2,1,0:T(1,128)S(1)}, u32[]{:S(2)}, u32[]{:S(2)}) %all-to-all-start.8) | async-done | bytes 24608 | tf_op jit(solution)/shard_map/all_to_all | solution.py:503
  145.0 0.7 collect.1
  145.7 0.0 copy-done.17
  145.7 0.0 copy-done.18
  145.7 0.0 copy-done.21
  145.7 0.0 copy-done.20
  145.8 0.0 copy-start.19
  145.8 0.3 conditional.1
  146.1 0.4 copy-done.19
  146.5 1.2 add_select_fusion.1
  (14 shorter events, 0.2 us)
Async XLA Ops:
  7.2 0.7 copy-start.10
  15.1 19.9 %all-to-all-start.4 = ((bf16[16,48,384]{2,1,0:T(8,128)(2,1)}), bf16[16,48,384]{2,1,0:T(8,128)(2,1)S(1)}, u32[]{:S(2)}, u32[]{:S(2)}) async-start(bf16[16,48,384]{2,1,0:T(8,128)(2,1)} %get-tuple-element.36), calls=%async_computation.5 | async-start | bytes 1179648 | tf_op jit(solution)/shard_map/all_to_all | solution.py:448
  35.0 0.8 copy-start.1
  35.8 31.7 %all-to-all-start.5 = ((bf16[8,4,64,512]{3,2,1,0:T(8,128)(2,1)}), bf16[8,4,64,512]{3,2,1,0:T(8,128)(2,1)S(1)}, u32[]{:S(2)}, u32[]{:S(2)}) async-start(bf16[8,4,64,512]{3,2,1,0:T(8,128)(2,1)} %bitcast.157), calls=%async_computation.6 | async-start | bytes 4194304 | tf_op jit(solution)/shard_map/all_to_all | solution.py:425
  40.3 1.1 copy-start.2
  41.3 1.0 copy-start.9
  42.4 49.1 %copy-start = (bf16[512,1024]{1,0:T(8,128)(2,1)S(1)}, bf16[512,1024]{1,0:T(8,128)(2,1)}, u32[]{:S(2)}) copy-start(bf16[512,1024]{1,0:T(8,128)(2,1)} %constant.104.clone.along_x_ref.back_x_ref) | copy-start | bytes 3145732
  47.3 1.0 copy-start.3
  48.3 0.8 copy-start.6
  67.5 24.0 %copy-start.4 = (bf16[1024,512]{1,0:T(8,128)(2,1)S(1)}, bf16[1024,512]{1,0:T(8,128)(2,1)}, u32[]{:S(2)}) copy-start(bf16[1024,512]{1,0:T(8,128)(2,1)} %constant.103.clone.along_y_ref) | copy-start | bytes 3145732
  67.5 24.0 %copy-start.5 = (bf16[512,1024]{1,0:T(8,128)(2,1)S(1)}, bf16[512,1024]{1,0:T(8,128)(2,1)}, u32[]{:S(2)}) copy-start(bf16[512,1024]{1,0:T(8,128)(2,1)} %constant.105.clone.back_y_ref) | copy-start | bytes 3145732
  102.8 4.8 %copy-start.11 = (s32[8]{0:T(128)S(1)}, s32[8]{0:T(128)}, u32[]{:S(2)}) copy-start(s32[8]{0:T(128)} %sizes_ref.1) | copy-start | bytes 100
  102.8 4.9 %copy-start.22 = (s32[32]{0:T(128)S(1)}, s32[32]{0:T(128)}, u32[]{:S(2)}) copy-start(s32[32]{0:T(128)} %param.19) | copy-start | bytes 388
  102.8 23.8 %copy-start.7 = (f32[24,6656]{1,0:T(8,128)S(1)}, f32[24,6656]{1,0:T(8,128)}, u32[]{:S(2)}) copy-start(f32[24,6656]{1,0:T(8,128)} %copy-done.6) | copy-start | bytes 1916932
  102.8 23.8 %copy-start.8 = (bf16[256,1024]{1,0:T(8,128)(2,1)S(1)}, bf16[256,1024]{1,0:T(8,128)(2,1)}, u32[]{:S(2)}) copy-start(bf16[256,1024]{1,0:T(8,128)(2,1)} %constant.106.clone.table_ref) | copy-start | bytes 1572868
  102.8 23.8 %all-to-all-start.7 = ((bf16[128,8,512]{2,1,0:T(8,128)(2,1)}), bf16[128,8,512]{2,1,0:T(8,128)(2,1)S(1)}, u32[]{:S(2)}, u32[]{:S(2)}) async-start(bf16[128,8,512]{2,1,0:T(8,128)(2,1)} %bitcast.52), calls=%async_computation.8 | async-start | bytes 2097152 | tf_op jit(solution)/shard_map/all_to_all | solution.py:491
  107.7 38.1 %copy-start.20 = (pred[2048]{0:T(1024)(128)(4,1)}, pred[2048]{0:T(1024)(128)(4,1)S(1)}, u32[]{:S(2)}) copy-start(pred[2048]{0:T(1024)(128)(4,1)S(1)} %lt.82) | copy-start | bytes 6148
  109.4 2.6 %collective-permute-start = (bf16[128,256]{1,0:T(8,128)(2,1)S(1)}, bf16[128,256]{1,0:T(8,128)(2,1)S(1)}, u32[]{:S(2)}, u32[]{:S(2)}) collective-permute-start(bf16[128,256]{1,0:T(8,128)(2,1)S(1)} %maximum_bitcast_fusion.2), channel_id=1, source_target_pairs={{0,16},{16,32},{32,48},{48,64},{64,80},{80,96},{96,112},{1,17},{17... | collective-permute-start | bytes 196616 | tf_op jit(solution)/shard_map/ppermute | solution.py:521
  110.7 4.3 %collective-permute-start.1 = (bf16[128,256]{1,0:T(8,128)(2,1)S(1)}, bf16[128,256]{1,0:T(8,128)(2,1)S(1)}, u32[]{:S(2)}, u32[]{:S(2)}) collective-permute-start(bf16[128,256]{1,0:T(8,128)(2,1)S(1)} %maximum_bitcast_fusion.2), channel_id=1, source_target_pairs={{16,0},{32,16},{48,32},{64,48},{80,64},{96,80},{112,96},{17,1},{33... | collective-permute-start | bytes 196616 | tf_op jit(solution)/shard_map/ppermute | solution.py:522
  131.5 13.5 %all-to-all-start.8 = ((f32[16,1,384]{2,1,0:T(1,128)}), f32[16,1,384]{2,1,0:T(1,128)S(1)}, u32[]{:S(2)}, u32[]{:S(2)}) async-start(f32[16,1,384]{2,1,0:T(1,128)} %copy.122), calls=%async_computation.9 | async-start | bytes 49152 | tf_op jit(solution)/shard_map/all_to_all | solution.py:503
  137.4 8.3 %copy-start.17 = (f32[27,2048]{1,0:T(8,128)S(1)}, f32[27,2048]{1,0:T(8,128)}, u32[]{:S(2)}) copy-start(f32[27,2048]{1,0:T(8,128)} %stencil_ref.1) | copy-start | bytes 663556
  137.4 8.3 %copy-start.18 = (s32[3,2048]{1,0:T(4,128)S(1)}, s32[3,2048]{1,0:T(4,128)}, u32[]{:S(2)}) copy-start(s32[3,2048]{1,0:T(4,128)} %corner_ref.1) | copy-start | bytes 73732
  137.5 8.3 %copy-start.21 = (bf16[2048]{0:T(1024)(128)(2,1)S(1)}, bf16[2048]{0:T(1024)(128)(2,1)}, u32[]{:S(2)}) copy-start(bf16[2048]{0:T(1024)(128)(2,1)} %param.15) | copy-start | bytes 12292
  145.8 0.7 copy-start.19
where the time goes:
time: 155 us
  waiting for transfers between devices  41.5 us (27%)
  Pallas kernels  28.3 us (18%)
  starting transfers between devices  25.7 us (17%)
  blocking collectives  24 us (15%)
  between operations  14.2 us (9%)
  local copies, waits for them, and re-layouts  13.1 us (8%)
  other arithmetic  3.91 us (3%)
  matrix products  3.4 us (2%)
    all_to_all x1, blocking collectives, far_field_blocks(): lax.all_to_all(section.reshape(DEVS, 8, 2 * M), ('clus', 'pen'), 0, 0, ti...  24 us
    all_to_all x1, waiting for transfers between devices, far_field_blocks(): green = lax.all_to_all(green, 'clus', 0, 0, tiled=True)  18.4 us
    pallas_call x1, Pallas kernels, far_field_blocks(): pl.pallas_call(convolve_kernel, grid=(4,), out_shape=struct((2 * L, 2 * M...  11.3 us
    all_to_all x1, waiting for transfers between devices, far_field_blocks(): lax.all_to_all(section.reshape(DEVS, 8, 2 * M), ('clus', 'pen'), 0, 0, ti...  11 us
    all_to_all x1, starting transfers between devices, far_field_blocks(): recv = lax.all_to_all(sent, 'pen', 0, 0, tiled=True)  7.96 us
    pallas_call x1, Pallas kernels, far_field_blocks(): pl.pallas_call(bucket_kernel, out_shape=[struct((PENS, ROWS, SLOTS), bf16...  7.24 us
    all_to_all x1, waiting for transfers between devices, far_field_blocks(): recv = lax.all_to_all(sent, 'pen', 0, 0, tiled=True)  6.85 us
    unnamed x38, local copies, waits for them, and re-layouts  6.41 us
  transfers between devices with their start and end apart: 6, of which 5 were waited for; matrix products, arithmetic and copies ran while one was open for 8% of the time, Pallas kernels for 3%

commit v1 on v0

--- a/solution.py
+++ b/solution.py
@@ -18,7 +18,7 @@
 PENS = 16
 DEVS = 128
 ROOM = PENS * SLOTS + 512
-TILE = 256
+TILE = 512
 ROWS = 48
 FIELDS = 24
 
@@ -62,9 +62,8 @@
     slab_charge = (
         jnp.zeros((planes * M * M,), f32).at[slab_cell.reshape(-1)].add(deposit.reshape(-1))
     )
-    grid_block = lax.psum_scatter(
-        slab_charge.reshape(planes, M, M), "pen", scatter_dimension=1, tiled=True
-    )
+    grid_block = slab_charge.reshape(planes, pen_count, rows_own, M).transpose(1, 0, 2, 3)
+    grid_block = lax.all_to_all(grid_block, "pen", 0, 0, tiled=True).sum(axis=0)
     section = jnp.einsum("xyz,zdk->dxyk", grid_block, forward_table[0], precision=exact)
     section = (
         section.reshape(2, planes, rows_own, pen_count, pen_spread)
@@ -98,7 +97,8 @@
     lines = jnp.einsum("ckw,czk->zw", section, inverse_table[:, :, 0, :], precision=exact)
     lines = lines * (1.0 / (L * L * L))
     block = lines.reshape(M, rows_own, planes).transpose(2, 1, 0)
-    slab = lax.all_gather(block, "pen", axis=1, tiled=True)
+    slab = jnp.broadcast_to(block[None], (pen_count,) + block.shape)
+    slab = lax.all_to_all(slab, "pen", 0, 0, tiled=True).transpose(1, 0, 2, 3)
     return jnp.sum(stencil * slab.reshape(-1)[slab_cell], axis=0)
 
 
@@ -239,8 +239,13 @@
         out_ref[p] = (total_ref[ROWS * p : ROWS * p + ROWS, :] + extra).astype(bf16)
 
 
+def rows_as_bf16():
+    return iota((M, TILE), 0).astype(f32).astype(bf16)
+
+
 def hot_z(z, c):
-    return jnp.where(iota((M, TILE), 0) == z + c, 1.0, 0.0).astype(bf16)
+    one = jnp.ones((M, TILE), bf16)
+    return jnp.where(rows_as_bf16() == (z + c).astype(f32).astype(bf16), one, jnp.zeros_like(one))
 
 
 def deposit_kernel(
@@ -273,17 +278,18 @@
         y = fields[19:20].astype(jnp.int32)
         z = fields[20:21].astype(jnp.int32)
         weights = fields[0:18] * fields[18:19]
-        away = iota((M, TILE), 0) - y
-        is0, is1, is2 = away == 0, away == 1, away == 2
+        high = weights.astype(bf16)
+        low = (weights - high.astype(f32)).astype(bf16)
+        place = rows_as_bf16()
+        at0, at1, at2 = [place == (y + b).astype(f32).astype(bf16) for b in range(3)]
+        zero = jnp.zeros((M, TILE), bf16)
         for c in range(3):
             left_ref[:, c * TILE : (c + 1) * TILE] = hot_z(z, c)
             for xp in range(2):
-                w = [weights[xp * 9 + b * 3 + c : xp * 9 + b * 3 + c + 1] for b in range(3)]
-                v = jnp.where(is0, w[0], jnp.where(is1, w[1], jnp.where(is2, w[2], 0.0)))
-                high = v.astype(bf16)
-                low = (v - high.astype(f32)).astype(bf16)
-                right_ref[xp * M : (xp + 1) * M, c * TILE : (c + 1) * TILE] = high
-                low_ref[xp * M : (xp + 1) * M, c * TILE : (c + 1) * TILE] = low
+                for part, ref in ((high, right_ref), (low, low_ref)):
+                    w = [part[xp * 9 + b * 3 + c : xp * 9 + b * 3 + c + 1] for b in range(3)]
+                    v = jnp.where(at0, w[0], jnp.where(at1, w[1], jnp.where(at2, w[2], zero)))
+                    ref[xp * M : (xp + 1) * M, c * TILE : (c + 1) * TILE] = v
         left = left_ref[...]
         grid_ref[...] += lax.dot_general(
             left, right_ref[...], NT, preferred_element_type=f32
@@ -303,8 +309,15 @@
         ).astype(bf16)
 
 
+def recut_kernel(slab_ref, green_ref, *out_refs):
+    for s, ref in enumerate(out_refs):
+        first = (slab_ref[0] + s) % 8 * 4
+        for c in range(4):
+            ref[c] = green_ref[pl.ds(first + c, L // 8, stride=32), :].astype(bf16)
+
+
 def convolve_kernel(
-    recv_ref, green_ref, along_y_ref, along_x_ref, back_y_ref, back_x_ref, out_ref, in_ref, sum_ref
+    slab_ref, recv_ref, g0_ref, g1_ref, g2_ref, g3_ref, g4_ref, g5_ref, g6_ref, g7_ref, along_y_ref, along_x_ref, back_y_ref, back_x_ref, out_ref, in_ref, sum_ref, green_ref
 ):
     j = pl.program_id(0)
 
@@ -312,6 +325,9 @@
     def _():
         for h in range(4):
             in_ref[h] = recv_ref[:, h * 128 : h * 128 + 128].astype(f32)
+
+    for s, ref in enumerate((g0_ref, g1_ref, g2_ref, g3_ref, g4_ref, g5_ref, g6_ref, g7_ref)):
+        green_ref[(slab_ref[0] + 8 - s) % 8] = ref[0]
 
     def piece(xp):
         return jnp.concatenate(
@@ -419,10 +435,8 @@
 
 def far_field_blocks(charges, stencil, corner_cells, cluster_sizes, green_spectrum):
     along_z, along_y, along_x, back_y, back_x, back_z = [jnp.asarray(t) for t in tables()]
-    green = (
-        green_spectrum.astype(bf16).transpose(2, 1, 0).reshape(8, 4, L // 8, L)
-    )
-    green = lax.all_to_all(green, "clus", 0, 0, tiled=True)
+    slab = lax.axis_index("clus").astype(jnp.int32).reshape(1)
+    green = green_spectrum.transpose(1, 2, 0).reshape(-1, L)
     sent, route = pl.pallas_call(
         bucket_kernel,
         out_shape=[
@@ -439,13 +453,27 @@
         compiler_params=LIMIT,
         name="bucket",
     )(
-        lax.axis_index("clus").astype(jnp.int32).reshape(1),
+        slab,
         cluster_sizes,
         charges.reshape(8, CAP),
         stencil,
         corner_cells,
     )
+    green, sent = lax.optimization_barrier((green, sent))
+    pieces = pl.pallas_call(
+        recut_kernel,
+        grid=(4,),
+        out_shape=[struct((4, L // 8, L), bf16)] * 8,
+        in_specs=[SMEM, pl.BlockSpec((L // 8 * 32, 128), lambda j: (0, j))],
+        out_specs=[pl.BlockSpec((4, L // 8, 128), lambda j: (0, 0, j))] * 8,
+        compiler_params=LIMIT,
+        name="recut",
+    )(slab, green)
     recv = lax.all_to_all(sent, "pen", 0, 0, tiled=True)
+    pieces = [pieces[0]] + [
+        lax.ppermute(pieces[s], "clus", [(a, (a + s) % 8) for a in range(8)])
+        for s in range(1, 8)
+    ]
     section, packed, meta = pl.pallas_call(
         deposit_kernel,
         out_shape=[
@@ -464,7 +492,7 @@
         compiler_params=LIMIT,
         name="deposit",
     )(recv, along_z)
-    section, green = lax.optimization_barrier((section, green))
+    section, *pieces = lax.optimization_barrier((section, *pieces))
     section = lax.all_to_all(
         section.reshape(DEVS, 8, 2 * M), ("clus", "pen"), 0, 0, tiled=True
     )
@@ -473,8 +501,11 @@
         grid=(4,),
         out_shape=struct((2 * L, 2 * M), bf16),
         in_specs=[
+            SMEM,
             pl.BlockSpec((2 * L, 2 * M), lambda j: (0, 0)),
-            pl.BlockSpec((8, 1, L // 8, L), lambda j: (0, j, 0, 0)),
+        ]
+        + [pl.BlockSpec((1, L // 8, L), lambda j: (j, 0, 0))] * 8
+        + [
             pl.BlockSpec((2 * L, 2 * M), lambda j: (0, 0)),
             pl.BlockSpec((2 * M, 2 * L), lambda j: (0, 0)),
             pl.BlockSpec((2 * M, 2 * L), lambda j: (0, 0)),
@@ -484,10 +515,11 @@
         scratch_shapes=[
             pltpu.VMEM((4, 2 * L, 128), f32),
             pltpu.VMEM((4, 2 * L, 128), f32),
+            pltpu.VMEM((8, L // 8, L), bf16),
         ],
         compiler_params=LIMIT,
         name="convolve",
-    )(section.reshape(2 * L, 2 * M), green, along_y, along_x, back_y, back_x)
+    )(slab, section.reshape(2 * L, 2 * M), *pieces, along_y, along_x, back_y, back_x)
     section = lax.all_to_all(
         section.reshape(DEVS, 8, 2 * M), ("clus", "pen"), 0, 0, tiled=True
     )

time: 155 us -> 142 us (0.916)
  waiting for transfers between devices: 41.5 us -> 24.3 us
  between operations: 14.2 us -> 0.87 us
  starting transfers between devices: 25.7 us -> 34.9 us
  blocking collectives: 24 us -> 29.7 us
  Pallas kernels: 28.3 us -> 33.1 us
  other arithmetic: 3.91 us -> 1.48 us
    all_to_all x1 -> x0, waiting for transfers between devices: 18.4 us -> none  [far_field_blocks(): green = lax.all_to_all(green, 'clus', 0, 0, tiled=True)]
    ppermute x0 -> x7, starting transfers between devices: none -> 14 us  [far_field_blocks(): lax.ppermute(pieces[s], 'clus', [(a, (a + s) % 8) for a in range(8)])]
    ppermute x0 -> x7, waiting for transfers between devices: none -> 6.93 us  [far_field_blocks(): lax.ppermute(pieces[s], 'clus', [(a, (a + s) % 8) for a in range(8)])]
    all_to_all x1, waiting for transfers between devices: 6.85 us -> 0.01 us  [far_field_blocks(): recv = lax.all_to_all(sent, 'pen', 0, 0, tiled=True)]
    all_to_all x1, blocking collectives: 24 us -> 29.7 us  [far_field_blocks(): lax.all_to_all(section.reshape(DEVS, 8, 2 * M), ('clus', 'pen'), 0, 0, ti...]
    pallas_call x0 -> x1, Pallas kernels: none -> 5.39 us  [far_field_blocks(): pl.pallas_call(recut_kernel, grid=(4,), out_shape=[struct((4, L // 8, L),...]
    all_to_all x1 -> x0, starting transfers between devices: 4.47 us -> none  [far_field_blocks(): green = lax.all_to_all(green, 'clus', 0, 0, tiled=True)]
    unnamed x38, local copies, waits for them, and re-layouts: 6.41 us -> 9.64 us
  transfers between devices with their start and end apart: 6 -> 12, of which waited for: 5 -> 9; matrix products, arithmetic and copies ran while one was open for 8% -> 4% of each run, Pallas kernels for 3% -> 6%
where the time goes in v1:
time: 142 us; the launch traced here: 141 us
  starting transfers between devices  34.9 us (25%)
  Pallas kernels  33.1 us (23%)
  blocking collectives  29.7 us (21%)
  waiting for transfers between devices  24.3 us (17%)
  local copies, waits for them, and re-layouts  13.4 us (9%)
  matrix products  3.36 us (2%)
  other arithmetic  1.48 us (1%)
    all_to_all x1, blocking collectives, far_field_blocks(): lax.all_to_all(section.reshape(DEVS, 8, 2 * M), ('clus', 'pen'), 0, 0, ti...  29.7 us
    ppermute x7, starting transfers between devices, far_field_blocks(): lax.ppermute(pieces[s], 'clus', [(a, (a + s) % 8) for a in range(8)])  14 us
    pallas_call x1, Pallas kernels, far_field_blocks(): pl.pallas_call(convolve_kernel, grid=(4,), out_shape=struct((2 * L, 2 * M...  12.2 us
    all_to_all x1, waiting for transfers between devices, far_field_blocks(): lax.all_to_all(section.reshape(DEVS, 8, 2 * M), ('clus', 'pen'), 0, 0, ti...  12 us
    unnamed x38, local copies, waits for them, and re-layouts  9.64 us
    all_to_all x1, starting transfers between devices, far_field_blocks(): recv = lax.all_to_all(sent, 'pen', 0, 0, tiled=True)  8.09 us
    pallas_call x1, Pallas kernels, far_field_blocks(): pl.pallas_call(bucket_kernel, out_shape=[struct((PENS, ROWS, SLOTS), bf16...  7.23 us
    ppermute x7, waiting for transfers between devices, far_field_blocks(): lax.ppermute(pieces[s], 'clus', [(a, (a + s) % 8) for a in range(8)])  6.93 us
  transfers between devices with their start and end apart: 12, of which 9 were waited for; matrix products, arithmetic and copies ran while one was open for 4% of the time, Pallas kernels for 6%

profile of v1, /device:TPU:0, one launch (start us, length us, event | category | flops | bytes accessed | tf_op | source)
XLA Modules:
  0.0 141.1 jit_solution(17290171648634290983)
XLA Ops:
  0.0 0.7 reshape.517.charge_ref
  0.7 0.7 copy-done.11
  1.4 7.2 %bucket.1 = (bf16[16,48,384]{2,1,0:T(8,128)(2,1)}, s32[8,2048]{1,0:T(8,128)S(1)}) custom-call(s32[1]{0:T(128)} %bitcast.51.slab_ref, s32[8]{0:T(128)S(1)} %copy-done.11, bf16[8,256]{1,0:T(8,128)(2,1)S(1)} %reshape.517.charge_ref, f32[27,2048]{1,0:T(8,128)} %stencil_ref.1, s32[3,2048]{1,0:T(4,128)} %corner_ref.1), custom_call_target="tpu_custom_call" | custom-call | tf_op jit(solution)/shard_map/bucket/pallas_call | solution.py:440
  8.6 8.1 %all-to-all-start.6 = ((bf16[16,48,384]{2,1,0:T(8,128)(2,1)}), bf16[16,48,384]{2,1,0:T(8,128)(2,1)S(1)}, u32[]{:S(2)}, u32[]{:S(2)}) async-start(bf16[16,48,384]{2,1,0:T(8,128)(2,1)} %get-tuple-element.54), calls=%async_computation.6 | async-start | bytes 1179648 | tf_op jit(solution)/shard_map/all_to_all | solution.py:472
  16.7 5.4 %recut.1 = (bf16[4,64,512]{2,1,0:T(8,128)(2,1)S(1)}, bf16[4,64,512]{2,1,0:T(8,128)(2,1)S(1)}, bf16[4,64,512]{2,1,0:T(8,128)(2,1)S(1)}, bf16[4,64,512]{2,1,0:T(8,...) custom-call(s32[1]{0:T(128)} %bitcast.51.slab_ref, ...), custom_call_target="tpu_custom_call" | custom-call | tf_op jit(solution)/shard_map/recut/pallas_call | solution.py:463
  22.1 0.7 copy-done.5
  22.8 0.0 collective-permute-start
  22.8 1.6 %collective-permute-start.1 = (bf16[4,64,512]{2,1,0:T(8,128)(2,1)S(1)}, bf16[4,64,512]{2,1,0:T(8,128)(2,1)S(1)}, u32[]{:S(2)}, u32[]{:S(2)}) collective-permute-start(bf16[4,64,512]{2,1,0:T(8,128)(2,1)S(1)} %get-tuple-element.60), channel_id=1, source_target_pairs={{0,32},{16,48},{32,64},{48,80},{64,96},{80,112},{96,0},{112,16},{1... | collective-permute-start | bytes 786440 | tf_op jit(solution)/shard_map/ppermute | solution.py:474
  24.4 2.3 %collective-permute-start.2 = (bf16[4,64,512]{2,1,0:T(8,128)(2,1)}, bf16[4,64,512]{2,1,0:T(8,128)(2,1)}, u32[]{:S(2)}, u32[]{:S(2)}) collective-permute-start(bf16[4,64,512]{2,1,0:T(8,128)(2,1)} %get-tuple-element.61), channel_id=1, source_target_pairs={{0,48},{16,64},{32,80},{48,96},{64,112},{80,0},{96,16},{112,32},{1... | collective-permute-start | bytes 786440 | tf_op jit(solution)/shard_map/ppermute | solution.py:474
  26.6 1.8 %collective-permute-start.3 = (bf16[4,64,512]{2,1,0:T(8,128)(2,1)}, bf16[4,64,512]{2,1,0:T(8,128)(2,1)}, u32[]{:S(2)}, u32[]{:S(2)}) collective-permute-start(bf16[4,64,512]{2,1,0:T(8,128)(2,1)} %get-tuple-element.62), channel_id=1, source_target_pairs={{0,64},{16,80},{32,96},{48,112},{64,0},{80,16},{96,32},{112,48},{1... | collective-permute-start | bytes 786440 | tf_op jit(solution)/shard_map/ppermute | solution.py:474
  28.5 1.8 %collective-permute-start.4 = (bf16[4,64,512]{2,1,0:T(8,128)(2,1)}, bf16[4,64,512]{2,1,0:T(8,128)(2,1)}, u32[]{:S(2)}, u32[]{:S(2)}) collective-permute-start(bf16[4,64,512]{2,1,0:T(8,128)(2,1)} %get-tuple-element.63), channel_id=1, source_target_pairs={{0,80},{16,96},{32,112},{48,0},{64,16},{80,32},{96,48},{112,64},{1... | collective-permute-start | bytes 786440 | tf_op jit(solution)/shard_map/ppermute | solution.py:474
  30.3 1.8 %collective-permute-done.g1_ref = bf16[4,64,512]{2,1,0:T(8,128)(2,1)S(1)} collective-permute-done((bf16[4,64,512]{2,1,0:T(8,128)(2,1)S(1)}, bf16[4,64,512]{2,1,0:T(8,128)(2,1)S(1)}, u32[]{:S(2)}, u32[]{:S(2)}) %collective-permute-start) | collective-permute-done | bytes 262176 | tf_op jit(solution)/shard_map/ppermute | solution.py:474
  32.0 0.7 copy-done.7
  32.7 1.8 %collective-permute-start.5 = (bf16[4,64,512]{2,1,0:T(8,128)(2,1)}, bf16[4,64,512]{2,1,0:T(8,128)(2,1)}, u32[]{:S(2)}, u32[]{:S(2)}) collective-permute-start(bf16[4,64,512]{2,1,0:T(8,128)(2,1)} %get-tuple-element.64), channel_id=1, source_target_pairs={{0,96},{16,112},{32,0},{48,16},{64,32},{80,48},{96,64},{112,80},{1... | collective-permute-start | bytes 786440 | tf_op jit(solution)/shard_map/ppermute | solution.py:474
  34.6 0.0 collective-permute-done.1.g2_ref
  34.6 0.7 copy-done.9
  35.3 4.7 %collective-permute-start.6 = (bf16[4,64,512]{2,1,0:T(8,128)(2,1)}, bf16[4,64,512]{2,1,0:T(8,128)(2,1)}, u32[]{:S(2)}, u32[]{:S(2)}) collective-permute-start(bf16[4,64,512]{2,1,0:T(8,128)(2,1)} %get-tuple-element.65), channel_id=1, source_target_pairs={{0,112},{16,0},{32,16},{48,32},{64,48},{80,64},{96,80},{112,96},{1... | collective-permute-start | bytes 786440 | tf_op jit(solution)/shard_map/ppermute | solution.py:474
  40.0 0.0 all-to-all-done.6.recv_ref
  40.0 1.0 copy-done.4
  41.0 3.5 %deposit.1 = (bf16[1024,512]{1,0:T(8,128)(2,1)S(1)}, f32[24,6656]{1,0:T(8,128)S(1)}, s32[17]{0:T(128)S(1)}) custom-call(bf16[16,48,384]{2,1,0:T(8,128)(2,1)S(1)} %all-to-all-done.6.recv_ref, bf16[1024,256]{1,0:T(8,128)(2,1)S(1)} %copy-done.4), custom_call_target="tpu_custom_call" | custom-call | tf_op jit(solution)/shard_map/deposit/pallas_call | solution.py:477
  44.5 0.1 collective-permute-done.2.g3_ref
  44.6 1.1 collective-permute-done.3.g4_ref
  45.7 1.8 %collective-permute-done.4.g5_ref = bf16[4,64,512]{2,1,0:T(8,128)(2,1)} collective-permute-done((bf16[4,64,512]{2,1,0:T(8,128)(2,1)}, bf16[4,64,512]{2,1,0:T(8,128)(2,1)}, u32[]{:S(2)}, u32[]{:S(2)}) %collective-permute-start.4) | collective-permute-done | bytes 262176 | tf_op jit(solution)/shard_map/ppermute | solution.py:474
  47.5 0.4 collective-permute-done.5.g6_ref
  47.9 1.7 %collective-permute-done.6.g7_ref = bf16[4,64,512]{2,1,0:T(8,128)(2,1)} collective-permute-done((bf16[4,64,512]{2,1,0:T(8,128)(2,1)}, bf16[4,64,512]{2,1,0:T(8,128)(2,1)}, u32[]{:S(2)}, u32[]{:S(2)}) %collective-permute-start.6) | collective-permute-done | bytes 262176 | tf_op jit(solution)/shard_map/ppermute | solution.py:474
  49.7 29.7 %all_to_all.68 = bf16[128,8,512]{2,1,0:T(8,128)(2,1)S(1)} all-to-all(bf16[128,8,512]{2,1,0:T(8,128)(2,1)S(1)} %bitcast.149), channel_id=1, replica_groups=mesh['clus'=8,'pen'=16] {'clus','pen'}, dimensions={0} | all-to-all | bytes 2097152 | tf_op jit(solution)/shard_map/all_to_all | solution.py:496
  79.3 0.0 copy-done
  79.4 0.0 copy-done.1
  79.4 1.2 copy-done.2
  80.6 0.9 copy-done.6
  81.5 0.9 copy-done.8
  82.5 0.9 copy-done.10
  83.4 12.2 %convolve.1 = bf16[1024,512]{1,0:T(8,128)(2,1)} custom-call(s32[1]{0:T(128)} %bitcast.51.slab_ref, bf16[1024,512]{1,0:T(8,128)(2,1)S(1)} %bitcast.147, bf16[4,64,512]{2,1,0:T(8,128)(2,1)S(1)} %copy-done.6, bf16[4,64,512]{2,1,0:T(8,128)(2,1)S(1)} %copy-done.8, bf16[4,64,512]{2,1,0:T(8,128)(2,1)S(1)} %copy-done.10, ...), custom_call_target="tpu_custom_call" | custom-call | tf_op jit(solution)/shard_map/convolve/pallas_call | solution.py:499
  95.6 4.6 %all-to-all-start.8 = ((bf16[128,8,512]{2,1,0:T(8,128)(2,1)}), bf16[128,8,512]{2,1,0:T(8,128)(2,1)S(1)}, u32[]{:S(2)}, u32[]{:S(2)}) async-start(bf16[128,8,512]{2,1,0:T(8,128)(2,1)} %bitcast.54), calls=%async_computation.8 | async-start | bytes 2097152 | tf_op jit(solution)/shard_map/all_to_all | solution.py:523
  100.3 0.0 copy-done.12
  100.3 0.0 copy-start.18
  100.3 0.0 copy-start.21
  100.3 0.0 copy-start.23
  100.3 0.1 iota_compare_fusion
  100.4 0.6 lt.82
  101.0 0.0 copy-done.24
  101.1 1.3 collective-permute-start.7
  102.4 1.3 collective-permute-start.8
  103.7 0.0 collective-permute-done.7
  103.8 2.9 %collective-permute-done.8 = bf16[128,256]{1,0:T(8,128)(2,1)S(1)} collective-permute-done((bf16[128,256]{1,0:T(8,128)(2,1)S(1)}, bf16[128,256]{1,0:T(8,128)(2,1)S(1)}, u32[]{:S(2)}, u32[]{:S(2)}) %collective-permute-start.8) | collective-permute-done | bytes 65568 | tf_op jit(solution)/shard_map/ppermute | solution.py:554
  106.7 0.6 gather_fusion.1
  107.3 12.0 %all-to-all-done.8 = bf16[128,8,512]{2,1,0:T(8,128)(2,1)S(1)} async-done(((bf16[128,8,512]{2,1,0:T(8,128)(2,1)}), bf16[128,8,512]{2,1,0:T(8,128)(2,1)S(1)}, u32[]{:S(2)}, u32[]{:S(2)}) %all-to-all-start.8) | async-done | bytes 1048608 | tf_op jit(solution)/shard_map/all_to_all | solution.py:523
  119.3 1.0 copy-done.3
  120.4 4.1 %interpolate.1 = (f32[16,384]{1,0:T(8,128)S(1)}, f32[8,128]{1,0:T(8,128)S(1)}) custom-call(s32[17]{0:T(128)S(1)} %get-tuple-element.55.meta_ref, bf16[1024,512]{1,0:T(8,128)(2,1)S(1)} %bitcast.148, bf16[256,1024]{1,0:T(8,128)(2,1)S(1)} %copy-done.3, f32[24,6656]{1,0:T(8,128)S(1)} %get-tuple-element.75.packed_ref), custom_call_target="tpu_custom_call" | custom-call | tf_op jit(solution)/shard_map/interpolate/pallas_call | solution.py:526
  124.5 0.6 copy.144
  125.1 5.6 %all-to-all-start.9 = ((f32[16,1,384]{2,1,0:T(1,128)}), f32[16,1,384]{2,1,0:T(1,128)S(1)}, u32[]{:S(2)}, u32[]{:S(2)}) async-start(f32[16,1,384]{2,1,0:T(1,128)} %copy.144), calls=%async_computation.9 | async-start | bytes 49152 | tf_op jit(solution)/shard_map/all_to_all | solution.py:535
  130.7 3.4 %fusion.42 = f32[32,1,256]{2,1,0:T(1,128)S(1)} fusion(bf16[32,256,256]{2,1,0:T(8,128)(2,1)} %param.20, bf16[32,256,1]{1,0,2:T(8,128)(2,1)S(1)} %bitcast.170), kind=kOutput, calls=%fused_computation.78 | convolution fusion | flops 4194304 | bytes 4243456 | tf_op jit(solution)/shard_map/pjm,pm->pj/dot_general | solution.py:568
  134.2 0.6 copy.167
  134.8 0.5 slice.25
  135.9 2.4 %all-to-all-done.9 = f32[16,1,384]{2,1,0:T(1,128)S(1)} async-done(((f32[16,1,384]{2,1,0:T(1,128)}), f32[16,1,384]{2,1,0:T(1,128)S(1)}, u32[]{:S(2)}, u32[]{:S(2)}) %all-to-all-start.9) | async-done | bytes 24608 | tf_op jit(solution)/shard_map/all_to_all | solution.py:535
  138.4 0.7 collect.1
  139.0 0.0 copy-done.18
  139.0 0.0 copy-done.21
  139.0 0.0 copy-done.23
  139.1 0.0 copy-start.22
  139.1 0.6 conditional.1
  139.1 0.6 slice.17
  139.7 0.1 copy-done.22
  139.8 1.3 add_select_fusion.1
  (25 shorter events, 0.2 us)
Async XLA Ops:
  0.7 0.7 copy-start.11
  8.6 70.8 %copy-start = (bf16[512,1024]{1,0:T(8,128)(2,1)S(1)}, bf16[512,1024]{1,0:T(8,128)(2,1)}, u32[]{:S(2)}) copy-start(bf16[512,1024]{1,0:T(8,128)(2,1)} %constant.104.clone.along_x_ref.back_x_ref) | copy-start | bytes 3145732
  8.6 70.8 %copy-start.1 = (bf16[1024,512]{1,0:T(8,128)(2,1)S(1)}, bf16[1024,512]{1,0:T(8,128)(2,1)}, u32[]{:S(2)}) copy-start(bf16[1024,512]{1,0:T(8,128)(2,1)} %constant.103.clone.along_y_ref) | copy-start | bytes 3145732
  8.6 31.4 %all-to-all-start.6 = ((bf16[16,48,384]{2,1,0:T(8,128)(2,1)}), bf16[16,48,384]{2,1,0:T(8,128)(2,1)S(1)}, u32[]{:S(2)}, u32[]{:S(2)}) async-start(bf16[16,48,384]{2,1,0:T(8,128)(2,1)} %get-tuple-element.54), calls=%async_computation.6 | async-start | bytes 1179648 | tf_op jit(solution)/shard_map/all_to_all | solution.py:472
  22.1 0.7 copy-start.5
  22.8 9.3 %collective-permute-start = (bf16[4,64,512]{2,1,0:T(8,128)(2,1)S(1)}, bf16[4,64,512]{2,1,0:T(8,128)(2,1)S(1)}, u32[]{:S(2)}, u32[]{:S(2)}) collective-permute-start(bf16[4,64,512]{2,1,0:T(8,128)(2,1)S(1)} %get-tuple-element.59), channel_id=1, source_target_pairs={{0,16},{16,32},{32,48},{48,64},{64,80},{80,96},{96,112},{112,0},{1... | collective-permute-start | bytes 786440 | tf_op jit(solution)/shard_map/ppermute | solution.py:474
  22.8 11.8 %collective-permute-start.1 = (bf16[4,64,512]{2,1,0:T(8,128)(2,1)S(1)}, bf16[4,64,512]{2,1,0:T(8,128)(2,1)S(1)}, u32[]{:S(2)}, u32[]{:S(2)}) collective-permute-start(bf16[4,64,512]{2,1,0:T(8,128)(2,1)S(1)} %get-tuple-element.60), channel_id=1, source_target_pairs={{0,32},{16,48},{32,64},{48,80},{64,96},{80,112},{96,0},{112,16},{1... | collective-permute-start | bytes 786440 | tf_op jit(solution)/shard_map/ppermute | solution.py:474
  24.4 20.2 %collective-permute-start.2 = (bf16[4,64,512]{2,1,0:T(8,128)(2,1)}, bf16[4,64,512]{2,1,0:T(8,128)(2,1)}, u32[]{:S(2)}, u32[]{:S(2)}) collective-permute-start(bf16[4,64,512]{2,1,0:T(8,128)(2,1)} %get-tuple-element.61), channel_id=1, source_target_pairs={{0,48},{16,64},{32,80},{48,96},{64,112},{80,0},{96,16},{112,32},{1... | collective-permute-start | bytes 786440 | tf_op jit(solution)/shard_map/ppermute | solution.py:474
  26.6 19.1 %collective-permute-start.3 = (bf16[4,64,512]{2,1,0:T(8,128)(2,1)}, bf16[4,64,512]{2,1,0:T(8,128)(2,1)}, u32[]{:S(2)}, u32[]{:S(2)}) collective-permute-start(bf16[4,64,512]{2,1,0:T(8,128)(2,1)} %get-tuple-element.62), channel_id=1, source_target_pairs={{0,64},{16,80},{32,96},{48,112},{64,0},{80,16},{96,32},{112,48},{1... | collective-permute-start | bytes 786440 | tf_op jit(solution)/shard_map/ppermute | solution.py:474
  28.5 19.0 %collective-permute-start.4 = (bf16[4,64,512]{2,1,0:T(8,128)(2,1)}, bf16[4,64,512]{2,1,0:T(8,128)(2,1)}, u32[]{:S(2)}, u32[]{:S(2)}) collective-permute-start(bf16[4,64,512]{2,1,0:T(8,128)(2,1)} %get-tuple-element.63), channel_id=1, source_target_pairs={{0,80},{16,96},{32,112},{48,0},{64,16},{80,32},{96,48},{112,64},{1... | collective-permute-start | bytes 786440 | tf_op jit(solution)/shard_map/ppermute | solution.py:474
  32.0 0.7 copy-start.7
  32.7 15.2 %collective-permute-start.5 = (bf16[4,64,512]{2,1,0:T(8,128)(2,1)}, bf16[4,64,512]{2,1,0:T(8,128)(2,1)}, u32[]{:S(2)}, u32[]{:S(2)}) collective-permute-start(bf16[4,64,512]{2,1,0:T(8,128)(2,1)} %get-tuple-element.64), channel_id=1, source_target_pairs={{0,96},{16,112},{32,0},{48,16},{64,32},{80,48},{96,64},{112,80},{1... | collective-permute-start | bytes 786440 | tf_op jit(solution)/shard_map/ppermute | solution.py:474
  34.6 0.7 copy-start.9
  35.3 14.4 %collective-permute-start.6 = (bf16[4,64,512]{2,1,0:T(8,128)(2,1)}, bf16[4,64,512]{2,1,0:T(8,128)(2,1)}, u32[]{:S(2)}, u32[]{:S(2)}) collective-permute-start(bf16[4,64,512]{2,1,0:T(8,128)(2,1)} %get-tuple-element.65), channel_id=1, source_target_pairs={{0,112},{16,0},{32,16},{48,32},{64,48},{80,64},{96,80},{112,96},{1... | collective-permute-start | bytes 786440 | tf_op jit(solution)/shard_map/ppermute | solution.py:474
  40.0 1.0 copy-start.4
  79.4 1.2 copy-start.2
  80.6 0.9 copy-start.6
  81.5 0.9 copy-start.8
  82.5 0.9 copy-start.10
  83.4 16.9 %copy-start.12 = (s32[8]{0:T(128)S(1)}, s32[8]{0:T(128)}, u32[]{:S(2)}) copy-start(s32[8]{0:T(128)} %sizes_ref.1) | copy-start | bytes 100
  83.4 17.6 %copy-start.24 = (s32[32]{0:T(128)S(1)}, s32[32]{0:T(128)}, u32[]{:S(2)}) copy-start(s32[32]{0:T(128)} %param.19) | copy-start | bytes 388
  95.6 23.7 %all-to-all-start.8 = ((bf16[128,8,512]{2,1,0:T(8,128)(2,1)}), bf16[128,8,512]{2,1,0:T(8,128)(2,1)S(1)}, u32[]{:S(2)}, u32[]{:S(2)}) async-start(bf16[128,8,512]{2,1,0:T(8,128)(2,1)} %bitcast.54), calls=%async_computation.8 | async-start | bytes 2097152 | tf_op jit(solution)/shard_map/all_to_all | solution.py:523
  100.3 38.7 %copy-start.18 = (f32[27,2048]{1,0:T(8,128)S(1)}, f32[27,2048]{1,0:T(8,128)}, u32[]{:S(2)}) copy-start(f32[27,2048]{1,0:T(8,128)} %stencil_ref.1) | copy-start | bytes 663556
  100.3 38.7 %copy-start.21 = (s32[3,2048]{1,0:T(4,128)S(1)}, s32[3,2048]{1,0:T(4,128)}, u32[]{:S(2)}) copy-start(s32[3,2048]{1,0:T(4,128)} %corner_ref.1) | copy-start | bytes 73732
  100.3 38.7 %copy-start.23 = (bf16[2048]{0:T(1024)(128)(2,1)S(1)}, bf16[2048]{0:T(1024)(128)(2,1)}, u32[]{:S(2)}) copy-start(bf16[2048]{0:T(1024)(128)(2,1)} %param.15) | copy-start | bytes 12292
  101.1 2.6 %collective-permute-start.7 = (bf16[128,256]{1,0:T(8,128)(2,1)S(1)}, bf16[128,256]{1,0:T(8,128)(2,1)S(1)}, u32[]{:S(2)}, u32[]{:S(2)}) collective-permute-start(bf16[128,256]{1,0:T(8,128)(2,1)S(1)} %maximum_bitcast_fusion.2), channel_id=1, source_target_pairs={{0,16},{16,32},{32,48},{48,64},{64,80},{80,96},{96,112},{1,17},{17... | collective-permute-start | bytes 196616 | tf_op jit(solution)/shard_map/ppermute | solution.py:553
  102.4 4.3 %collective-permute-start.8 = (bf16[128,256]{1,0:T(8,128)(2,1)S(1)}, bf16[128,256]{1,0:T(8,128)(2,1)S(1)}, u32[]{:S(2)}, u32[]{:S(2)}) collective-permute-start(bf16[128,256]{1,0:T(8,128)(2,1)S(1)} %maximum_bitcast_fusion.2), channel_id=1, source_target_pairs={{16,0},{32,16},{48,32},{64,48},{80,64},{96,80},{112,96},{17,1},{33... | collective-permute-start | bytes 196616 | tf_op jit(solution)/shard_map/ppermute | solution.py:554
  119.3 1.0 copy-start.3
  125.1 13.2 %all-to-all-start.9 = ((f32[16,1,384]{2,1,0:T(1,128)}), f32[16,1,384]{2,1,0:T(1,128)S(1)}, u32[]{:S(2)}, u32[]{:S(2)}) async-start(f32[16,1,384]{2,1,0:T(1,128)} %copy.144), calls=%async_computation.9 | async-start | bytes 49152 | tf_op jit(solution)/shard_map/all_to_all | solution.py:535
  139.1 0.7 copy-start.22

commit v2 on v1

--- a/solution.py
+++ b/solution.py
@@ -327,38 +327,59 @@
             in_ref[h] = recv_ref[:, h * 128 : h * 128 + 128].astype(f32)
 
     for s, ref in enumerate((g0_ref, g1_ref, g2_ref, g3_ref, g4_ref, g5_ref, g6_ref, g7_ref)):
-        green_ref[(slab_ref[0] + 8 - s) % 8] = ref[0]
-
-    def piece(xp):
+        for i in range(2):
+            green_ref[i, (slab_ref[0] + 8 - s) % 8] = ref[i]
+
+    def piece(i, xp):
         return jnp.concatenate(
             [
-                in_ref[2 * xp + h, pl.ds(2 * j + c, DEVS, stride=8), :].astype(bf16)
+                in_ref[2 * xp + h, pl.ds(4 * j + 2 * i + c, DEVS, stride=8), :].astype(bf16)
                 for c in range(2)
                 for h in range(2)
             ],
             axis=1,
         )
 
-    field = jnp.concatenate([piece(0), piece(1)], axis=0)
-    part = lax.dot_general(along_y_ref[...], field, NT, preferred_element_type=f32).astype(bf16)
-    part = jnp.concatenate([part[:L], part[L:]], axis=1)
-    part = jnp.dot(part, along_x_ref[...], preferred_element_type=f32)
-    green = green_ref[...].reshape(L, L).astype(f32)
-    part = jnp.concatenate(
-        [(part[:, :L] * green).astype(bf16), (part[:, L:] * green).astype(bf16)], axis=0
-    )
-    part = jnp.dot(back_y_ref[...], part, preferred_element_type=f32).astype(bf16)
-    part = jnp.concatenate([part[:M], part[M:]], axis=1)
-    part = lax.dot_general(back_x_ref[...], part, NT, preferred_element_type=f32)
-    for c in range(2):
-        for xp in range(2):
-            row = c * M + xp * DEVS
-            for h in range(2):
-                sum_ref[2 * xp + h, pl.ds(2 * j + c, DEVS, stride=8), :] = part[
-                    row : row + DEVS, h * 128 : h * 128 + 128
-                ]
-
-    @pl.when(j == 3)
+    both = [jnp.concatenate([piece(i, 0), piece(i, 1)], axis=0) for i in range(2)]
+    both = [
+        lax.dot_general(along_y_ref[...], t, NT, preferred_element_type=f32).astype(bf16)
+        for t in both
+    ]
+    both = [
+        jnp.dot(
+            jnp.concatenate([t[:L], t[L:]], axis=1),
+            along_x_ref[...],
+            preferred_element_type=f32,
+        )
+        for t in both
+    ]
+    greens = [green_ref[i].reshape(L, L).astype(f32) for i in range(2)]
+    both = [
+        jnp.concatenate([(t[:, :L] * g).astype(bf16), (t[:, L:] * g).astype(bf16)], axis=0)
+        for t, g in zip(both, greens)
+    ]
+    both = [
+        jnp.dot(back_y_ref[...], t, preferred_element_type=f32).astype(bf16) for t in both
+    ]
+    both = [
+        lax.dot_general(
+            back_x_ref[...],
+            jnp.concatenate([t[:M], t[M:]], axis=1),
+            NT,
+            preferred_element_type=f32,
+        )
+        for t in both
+    ]
+    for i in range(2):
+        for c in range(2):
+            for xp in range(2):
+                row = c * M + xp * DEVS
+                for h in range(2):
+                    sum_ref[2 * xp + h, pl.ds(4 * j + 2 * i + c, DEVS, stride=8), :] = both[i][
+                        row : row + DEVS, h * 128 : h * 128 + 128
+                    ]
+
+    @pl.when(j == 1)
     def _():
         for h in range(4):
             out_ref[:, h * 128 : h * 128 + 128] = sum_ref[h].astype(bf16)
@@ -498,13 +519,13 @@
     )
     section = pl.pallas_call(
         convolve_kernel,
-        grid=(4,),
+        grid=(2,),
         out_shape=struct((2 * L, 2 * M), bf16),
         in_specs=[
             SMEM,
             pl.BlockSpec((2 * L, 2 * M), lambda j: (0, 0)),
         ]
-        + [pl.BlockSpec((1, L // 8, L), lambda j: (j, 0, 0))] * 8
+        + [pl.BlockSpec((2, L // 8, L), lambda j: (j, 0, 0))] * 8
         + [
             pl.BlockSpec((2 * L, 2 * M), lambda j: (0, 0)),
             pl.BlockSpec((2 * M, 2 * L), lambda j: (0, 0)),
@@ -515,7 +536,7 @@
         scratch_shapes=[
             pltpu.VMEM((4, 2 * L, 128), f32),
             pltpu.VMEM((4, 2 * L, 128), f32),
-            pltpu.VMEM((8, L // 8, L), bf16),
+            pltpu.VMEM((2, 8, L // 8, L), bf16),
         ],
         compiler_params=LIMIT,
         name="convolve",

time: 142 us -> 139 us (0.979)
  Pallas kernels: 33.1 us -> 30.5 us
    pallas_call x1, Pallas kernels: 12.2 us -> 9.78 us  [far_field_blocks(): pl.pallas_call(convolve_kernel, grid=(2,), out_shape=struct((2 * L, 2 * M...]
where the time goes in v2:
time: 139 us; the launch traced here: 138 us
  starting transfers between devices  35.1 us (25%)
  Pallas kernels  30.5 us (22%)
  blocking collectives  29.7 us (21%)
  waiting for transfers between devices  24.1 us (17%)
  local copies, waits for them, and re-layouts  13.4 us (10%)
  matrix products  3.36 us (2%)
  other arithmetic  1.48 us (1%)
    all_to_all x1, blocking collectives, far_field_blocks(): lax.all_to_all(section.reshape(DEVS, 8, 2 * M), ('clus', 'pen'), 0, 0, ti...  29.7 us
    ppermute x7, starting transfers between devices, far_field_blocks(): lax.ppermute(pieces[s], 'clus', [(a, (a + s) % 8) for a in range(8)])  14 us
    all_to_all x1, waiting for transfers between devices, far_field_blocks(): lax.all_to_all(section.reshape(DEVS, 8, 2 * M), ('clus', 'pen'), 0, 0, ti...  12 us
    pallas_call x1, Pallas kernels, far_field_blocks(): pl.pallas_call(convolve_kernel, grid=(2,), out_shape=struct((2 * L, 2 * M...  9.78 us
    unnamed x38, local copies, waits for them, and re-layouts  9.64 us
    all_to_all x1, starting transfers between devices, far_field_blocks(): recv = lax.all_to_all(sent, 'pen', 0, 0, tiled=True)  8.09 us
    pallas_call x1, Pallas kernels, far_field_blocks(): pl.pallas_call(bucket_kernel, out_shape=[struct((PENS, ROWS, SLOTS), bf16...  7.23 us
    ppermute x7, waiting for transfers between devices, far_field_blocks(): lax.ppermute(pieces[s], 'clus', [(a, (a + s) % 8) for a in range(8)])  6.92 us
  transfers between devices with their start and end apart: 12, of which 9 were waited for; matrix products, arithmetic and copies ran while one was open for 4% of the time, Pallas kernels for 6%

profile of v2, /device:TPU:0, one launch (start us, length us, event | category | flops | bytes accessed | tf_op | source)
XLA Modules:
  0.0 138.5 jit_solution(2582702197639795845)
XLA Ops:
  0.0 0.7 reshape.517.charge_ref
  0.7 0.7 copy-done.11
  1.4 7.2 %bucket.1 = (bf16[16,48,384]{2,1,0:T(8,128)(2,1)}, s32[8,2048]{1,0:T(8,128)S(1)}) custom-call(s32[1]{0:T(128)} %bitcast.51.slab_ref, s32[8]{0:T(128)S(1)} %copy-done.11, bf16[8,256]{1,0:T(8,128)(2,1)S(1)} %reshape.517.charge_ref, f32[27,2048]{1,0:T(8,128)} %stencil_ref.1, s32[3,2048]{1,0:T(4,128)} %corner_ref.1), custom_call_target="tpu_custom_call" | custom-call | tf_op jit(solution)/shard_map/bucket/pallas_call | solution.py:461
  8.6 8.1 %all-to-all-start.6 = ((bf16[16,48,384]{2,1,0:T(8,128)(2,1)}), bf16[16,48,384]{2,1,0:T(8,128)(2,1)S(1)}, u32[]{:S(2)}, u32[]{:S(2)}) async-start(bf16[16,48,384]{2,1,0:T(8,128)(2,1)} %get-tuple-element.54), calls=%async_computation.6 | async-start | bytes 1179648 | tf_op jit(solution)/shard_map/all_to_all | solution.py:493
  16.7 5.4 %recut.1 = (bf16[4,64,512]{2,1,0:T(8,128)(2,1)S(1)}, bf16[4,64,512]{2,1,0:T(8,128)(2,1)S(1)}, bf16[4,64,512]{2,1,0:T(8,128)(2,1)S(1)}, bf16[4,64,512]{2,1,0:T(8,...) custom-call(s32[1]{0:T(128)} %bitcast.51.slab_ref, ...), custom_call_target="tpu_custom_call" | custom-call | tf_op jit(solution)/shard_map/recut/pallas_call | solution.py:484
  22.1 0.7 copy-done.5
  22.8 0.0 collective-permute-start
  22.8 1.6 %collective-permute-start.1 = (bf16[4,64,512]{2,1,0:T(8,128)(2,1)S(1)}, bf16[4,64,512]{2,1,0:T(8,128)(2,1)S(1)}, u32[]{:S(2)}, u32[]{:S(2)}) collective-permute-start(bf16[4,64,512]{2,1,0:T(8,128)(2,1)S(1)} %get-tuple-element.60), channel_id=1, source_target_pairs={{0,32},{16,48},{32,64},{48,80},{64,96},{80,112},{96,0},{112,16},{1... | collective-permute-start | bytes 786440 | tf_op jit(solution)/shard_map/ppermute | solution.py:495
  24.4 2.3 %collective-permute-start.2 = (bf16[4,64,512]{2,1,0:T(8,128)(2,1)}, bf16[4,64,512]{2,1,0:T(8,128)(2,1)}, u32[]{:S(2)}, u32[]{:S(2)}) collective-permute-start(bf16[4,64,512]{2,1,0:T(8,128)(2,1)} %get-tuple-element.61), channel_id=1, source_target_pairs={{0,48},{16,64},{32,80},{48,96},{64,112},{80,0},{96,16},{112,32},{1... | collective-permute-start | bytes 786440 | tf_op jit(solution)/shard_map/ppermute | solution.py:495
  26.6 1.8 %collective-permute-start.3 = (bf16[4,64,512]{2,1,0:T(8,128)(2,1)}, bf16[4,64,512]{2,1,0:T(8,128)(2,1)}, u32[]{:S(2)}, u32[]{:S(2)}) collective-permute-start(bf16[4,64,512]{2,1,0:T(8,128)(2,1)} %get-tuple-element.62), channel_id=1, source_target_pairs={{0,64},{16,80},{32,96},{48,112},{64,0},{80,16},{96,32},{112,48},{1... | collective-permute-start | bytes 786440 | tf_op jit(solution)/shard_map/ppermute | solution.py:495
  28.5 1.8 %collective-permute-start.4 = (bf16[4,64,512]{2,1,0:T(8,128)(2,1)}, bf16[4,64,512]{2,1,0:T(8,128)(2,1)}, u32[]{:S(2)}, u32[]{:S(2)}) collective-permute-start(bf16[4,64,512]{2,1,0:T(8,128)(2,1)} %get-tuple-element.63), channel_id=1, source_target_pairs={{0,80},{16,96},{32,112},{48,0},{64,16},{80,32},{96,48},{112,64},{1... | collective-permute-start | bytes 786440 | tf_op jit(solution)/shard_map/ppermute | solution.py:495
  30.3 1.8 %collective-permute-done.g1_ref = bf16[4,64,512]{2,1,0:T(8,128)(2,1)S(1)} collective-permute-done((bf16[4,64,512]{2,1,0:T(8,128)(2,1)S(1)}, bf16[4,64,512]{2,1,0:T(8,128)(2,1)S(1)}, u32[]{:S(2)}, u32[]{:S(2)}) %collective-permute-start) | collective-permute-done | bytes 262176 | tf_op jit(solution)/shard_map/ppermute | solution.py:495
  32.0 0.7 copy-done.7
  32.7 1.8 %collective-permute-start.5 = (bf16[4,64,512]{2,1,0:T(8,128)(2,1)}, bf16[4,64,512]{2,1,0:T(8,128)(2,1)}, u32[]{:S(2)}, u32[]{:S(2)}) collective-permute-start(bf16[4,64,512]{2,1,0:T(8,128)(2,1)} %get-tuple-element.64), channel_id=1, source_target_pairs={{0,96},{16,112},{32,0},{48,16},{64,32},{80,48},{96,64},{112,80},{1... | collective-permute-start | bytes 786440 | tf_op jit(solution)/shard_map/ppermute | solution.py:495
  34.6 0.0 collective-permute-done.1.g2_ref
  34.6 0.7 copy-done.9
  35.3 4.7 %collective-permute-start.6 = (bf16[4,64,512]{2,1,0:T(8,128)(2,1)}, bf16[4,64,512]{2,1,0:T(8,128)(2,1)}, u32[]{:S(2)}, u32[]{:S(2)}) collective-permute-start(bf16[4,64,512]{2,1,0:T(8,128)(2,1)} %get-tuple-element.65), channel_id=1, source_target_pairs={{0,112},{16,0},{32,16},{48,32},{64,48},{80,64},{96,80},{112,96},{1... | collective-permute-start | bytes 786440 | tf_op jit(solution)/shard_map/ppermute | solution.py:495
  40.0 0.0 all-to-all-done.6.recv_ref
  40.0 1.0 copy-done.4
  41.0 3.5 %deposit.1 = (bf16[1024,512]{1,0:T(8,128)(2,1)S(1)}, f32[24,6656]{1,0:T(8,128)S(1)}, s32[17]{0:T(128)S(1)}) custom-call(bf16[16,48,384]{2,1,0:T(8,128)(2,1)S(1)} %all-to-all-done.6.recv_ref, bf16[1024,256]{1,0:T(8,128)(2,1)S(1)} %copy-done.4), custom_call_target="tpu_custom_call" | custom-call | tf_op jit(solution)/shard_map/deposit/pallas_call | solution.py:498
  44.5 0.1 collective-permute-done.2.g3_ref
  44.6 1.1 collective-permute-done.3.g4_ref
  45.7 1.8 %collective-permute-done.4.g5_ref = bf16[4,64,512]{2,1,0:T(8,128)(2,1)} collective-permute-done((bf16[4,64,512]{2,1,0:T(8,128)(2,1)}, bf16[4,64,512]{2,1,0:T(8,128)(2,1)}, u32[]{:S(2)}, u32[]{:S(2)}) %collective-permute-start.4) | collective-permute-done | bytes 262176 | tf_op jit(solution)/shard_map/ppermute | solution.py:495
  47.5 0.4 collective-permute-done.5.g6_ref
  47.9 1.7 %collective-permute-done.6.g7_ref = bf16[4,64,512]{2,1,0:T(8,128)(2,1)} collective-permute-done((bf16[4,64,512]{2,1,0:T(8,128)(2,1)}, bf16[4,64,512]{2,1,0:T(8,128)(2,1)}, u32[]{:S(2)}, u32[]{:S(2)}) %collective-permute-start.6) | collective-permute-done | bytes 262176 | tf_op jit(solution)/shard_map/ppermute | solution.py:495
  49.7 29.7 %all_to_all.68 = bf16[128,8,512]{2,1,0:T(8,128)(2,1)S(1)} all-to-all(bf16[128,8,512]{2,1,0:T(8,128)(2,1)S(1)} %bitcast.149), channel_id=1, replica_groups=mesh['clus'=8,'pen'=16] {'clus','pen'}, dimensions={0} | all-to-all | bytes 2097152 | tf_op jit(solution)/shard_map/all_to_all | solution.py:517
  79.3 0.0 copy-done
  79.4 0.0 copy-done.1
  79.4 1.2 copy-done.2
  80.6 0.9 copy-done.6
  81.5 0.9 copy-done.8
  82.5 0.9 copy-done.10
  83.4 9.8 %convolve.1 = bf16[1024,512]{1,0:T(8,128)(2,1)} custom-call(s32[1]{0:T(128)} %bitcast.51.slab_ref, bf16[1024,512]{1,0:T(8,128)(2,1)S(1)} %bitcast.147, bf16[4,64,512]{2,1,0:T(8,128)(2,1)S(1)} %copy-done.6, bf16[4,64,512]{2,1,0:T(8,128)(2,1)S(1)} %copy-done.8, bf16[4,64,512]{2,1,0:T(8,128)(2,1)S(1)} %copy-done.10, ...), custom_call_target="tpu_custom_call" | custom-call | tf_op jit(solution)/shard_map/convolve/pallas_call | solution.py:520
  93.2 4.6 %all-to-all-start.8 = ((bf16[128,8,512]{2,1,0:T(8,128)(2,1)}), bf16[128,8,512]{2,1,0:T(8,128)(2,1)S(1)}, u32[]{:S(2)}, u32[]{:S(2)}) async-start(bf16[128,8,512]{2,1,0:T(8,128)(2,1)} %bitcast.54), calls=%async_computation.8 | async-start | bytes 2097152 | tf_op jit(solution)/shard_map/all_to_all | solution.py:544
  97.9 0.0 copy-done.12
  97.9 0.0 copy-start.18
  97.9 0.0 copy-start.21
  97.9 0.0 copy-start.23
  97.9 0.1 iota_compare_fusion
  98.0 0.6 lt.82
  98.6 0.0 copy-done.24
  98.7 1.3 collective-permute-start.7
  100.0 1.5 %collective-permute-start.8 = (bf16[128,256]{1,0:T(8,128)(2,1)S(1)}, bf16[128,256]{1,0:T(8,128)(2,1)S(1)}, u32[]{:S(2)}, u32[]{:S(2)}) collective-permute-start(bf16[128,256]{1,0:T(8,128)(2,1)S(1)} %maximum_bitcast_fusion.2), channel_id=1, source_target_pairs={{16,0},{32,16},{48,32},{64,48},{80,64},{96,80},{112,96},{17,1},{33... | collective-permute-start | bytes 196616 | tf_op jit(solution)/shard_map/ppermute | solution.py:575
  101.5 0.0 collective-permute-done.7
  101.5 2.8 %collective-permute-done.8 = bf16[128,256]{1,0:T(8,128)(2,1)S(1)} collective-permute-done((bf16[128,256]{1,0:T(8,128)(2,1)S(1)}, bf16[128,256]{1,0:T(8,128)(2,1)S(1)}, u32[]{:S(2)}, u32[]{:S(2)}) %collective-permute-start.8) | collective-permute-done | bytes 65568 | tf_op jit(solution)/shard_map/ppermute | solution.py:575
  104.3 0.6 gather_fusion.1
  104.9 12.0 %all-to-all-done.8 = bf16[128,8,512]{2,1,0:T(8,128)(2,1)S(1)} async-done(((bf16[128,8,512]{2,1,0:T(8,128)(2,1)}), bf16[128,8,512]{2,1,0:T(8,128)(2,1)S(1)}, u32[]{:S(2)}, u32[]{:S(2)}) %all-to-all-start.8) | async-done | bytes 1048608 | tf_op jit(solution)/shard_map/all_to_all | solution.py:544
  116.9 1.0 copy-done.3
  117.9 3.9 %interpolate.1 = (f32[16,384]{1,0:T(8,128)S(1)}, f32[8,128]{1,0:T(8,128)S(1)}) custom-call(s32[17]{0:T(128)S(1)} %get-tuple-element.55.meta_ref, bf16[1024,512]{1,0:T(8,128)(2,1)S(1)} %bitcast.148, bf16[256,1024]{1,0:T(8,128)(2,1)S(1)} %copy-done.3, f32[24,6656]{1,0:T(8,128)S(1)} %get-tuple-element.75.packed_ref), custom_call_target="tpu_custom_call" | custom-call | tf_op jit(solution)/shard_map/interpolate/pallas_call | solution.py:547
  121.9 0.6 copy.144
  122.5 5.6 %all-to-all-start.9 = ((f32[16,1,384]{2,1,0:T(1,128)}), f32[16,1,384]{2,1,0:T(1,128)S(1)}, u32[]{:S(2)}, u32[]{:S(2)}) async-start(f32[16,1,384]{2,1,0:T(1,128)} %copy.144), calls=%async_computation.9 | async-start | bytes 49152 | tf_op jit(solution)/shard_map/all_to_all | solution.py:556
  128.1 3.4 %fusion.42 = f32[32,1,256]{2,1,0:T(1,128)S(1)} fusion(bf16[32,256,256]{2,1,0:T(8,128)(2,1)} %param.20, bf16[32,256,1]{1,0,2:T(8,128)(2,1)S(1)} %bitcast.170), kind=kOutput, calls=%fused_computation.78 | convolution fusion | flops 4194304 | bytes 4243456 | tf_op jit(solution)/shard_map/pjm,pm->pj/dot_general | solution.py:589
  131.6 0.6 copy.167
  132.2 0.5 slice.25
  133.3 2.4 %all-to-all-done.9 = f32[16,1,384]{2,1,0:T(1,128)S(1)} async-done(((f32[16,1,384]{2,1,0:T(1,128)}), f32[16,1,384]{2,1,0:T(1,128)S(1)}, u32[]{:S(2)}, u32[]{:S(2)}) %all-to-all-start.9) | async-done | bytes 24608 | tf_op jit(solution)/shard_map/all_to_all | solution.py:556
  135.8 0.7 collect.1
  136.4 0.0 copy-done.18
  136.4 0.0 copy-done.21
  136.4 0.0 copy-done.23
  136.4 0.0 copy-start.22
  136.5 0.6 conditional.1
  136.5 0.6 slice.17
  137.1 0.1 copy-done.22
  137.1 1.3 add_select_fusion.1
  (25 shorter events, 0.2 us)
Async XLA Ops:
  0.7 0.7 copy-start.11
  8.6 70.8 %copy-start = (bf16[512,1024]{1,0:T(8,128)(2,1)S(1)}, bf16[512,1024]{1,0:T(8,128)(2,1)}, u32[]{:S(2)}) copy-start(bf16[512,1024]{1,0:T(8,128)(2,1)} %constant.104.clone.along_x_ref.back_x_ref) | copy-start | bytes 3145732
  8.6 70.8 %copy-start.1 = (bf16[1024,512]{1,0:T(8,128)(2,1)S(1)}, bf16[1024,512]{1,0:T(8,128)(2,1)}, u32[]{:S(2)}) copy-start(bf16[1024,512]{1,0:T(8,128)(2,1)} %constant.103.clone.along_y_ref) | copy-start | bytes 3145732
  8.6 31.4 %all-to-all-start.6 = ((bf16[16,48,384]{2,1,0:T(8,128)(2,1)}), bf16[16,48,384]{2,1,0:T(8,128)(2,1)S(1)}, u32[]{:S(2)}, u32[]{:S(2)}) async-start(bf16[16,48,384]{2,1,0:T(8,128)(2,1)} %get-tuple-element.54), calls=%async_computation.6 | async-start | bytes 1179648 | tf_op jit(solution)/shard_map/all_to_all | solution.py:493
  22.1 0.7 copy-start.5
  22.8 9.3 %collective-permute-start = (bf16[4,64,512]{2,1,0:T(8,128)(2,1)S(1)}, bf16[4,64,512]{2,1,0:T(8,128)(2,1)S(1)}, u32[]{:S(2)}, u32[]{:S(2)}) collective-permute-start(bf16[4,64,512]{2,1,0:T(8,128)(2,1)S(1)} %get-tuple-element.59), channel_id=1, source_target_pairs={{0,16},{16,32},{32,48},{48,64},{64,80},{80,96},{96,112},{112,0},{1... | collective-permute-start | bytes 786440 | tf_op jit(solution)/shard_map/ppermute | solution.py:495
  22.8 11.8 %collective-permute-start.1 = (bf16[4,64,512]{2,1,0:T(8,128)(2,1)S(1)}, bf16[4,64,512]{2,1,0:T(8,128)(2,1)S(1)}, u32[]{:S(2)}, u32[]{:S(2)}) collective-permute-start(bf16[4,64,512]{2,1,0:T(8,128)(2,1)S(1)} %get-tuple-element.60), channel_id=1, source_target_pairs={{0,32},{16,48},{32,64},{48,80},{64,96},{80,112},{96,0},{112,16},{1... | collective-permute-start | bytes 786440 | tf_op jit(solution)/shard_map/ppermute | solution.py:495
  24.4 20.2 %collective-permute-start.2 = (bf16[4,64,512]{2,1,0:T(8,128)(2,1)}, bf16[4,64,512]{2,1,0:T(8,128)(2,1)}, u32[]{:S(2)}, u32[]{:S(2)}) collective-permute-start(bf16[4,64,512]{2,1,0:T(8,128)(2,1)} %get-tuple-element.61), channel_id=1, source_target_pairs={{0,48},{16,64},{32,80},{48,96},{64,112},{80,0},{96,16},{112,32},{1... | collective-permute-start | bytes 786440 | tf_op jit(solution)/shard_map/ppermute | solution.py:495
  26.6 19.1 %collective-permute-start.3 = (bf16[4,64,512]{2,1,0:T(8,128)(2,1)}, bf16[4,64,512]{2,1,0:T(8,128)(2,1)}, u32[]{:S(2)}, u32[]{:S(2)}) collective-permute-start(bf16[4,64,512]{2,1,0:T(8,128)(2,1)} %get-tuple-element.62), channel_id=1, source_target_pairs={{0,64},{16,80},{32,96},{48,112},{64,0},{80,16},{96,32},{112,48},{1... | collective-permute-start | bytes 786440 | tf_op jit(solution)/shard_map/ppermute | solution.py:495
  28.5 19.0 %collective-permute-start.4 = (bf16[4,64,512]{2,1,0:T(8,128)(2,1)}, bf16[4,64,512]{2,1,0:T(8,128)(2,1)}, u32[]{:S(2)}, u32[]{:S(2)}) collective-permute-start(bf16[4,64,512]{2,1,0:T(8,128)(2,1)} %get-tuple-element.63), channel_id=1, source_target_pairs={{0,80},{16,96},{32,112},{48,0},{64,16},{80,32},{96,48},{112,64},{1... | collective-permute-start | bytes 786440 | tf_op jit(solution)/shard_map/ppermute | solution.py:495
  32.0 0.7 copy-start.7
  32.7 15.2 %collective-permute-start.5 = (bf16[4,64,512]{2,1,0:T(8,128)(2,1)}, bf16[4,64,512]{2,1,0:T(8,128)(2,1)}, u32[]{:S(2)}, u32[]{:S(2)}) collective-permute-start(bf16[4,64,512]{2,1,0:T(8,128)(2,1)} %get-tuple-element.64), channel_id=1, source_target_pairs={{0,96},{16,112},{32,0},{48,16},{64,32},{80,48},{96,64},{112,80},{1... | collective-permute-start | bytes 786440 | tf_op jit(solution)/shard_map/ppermute | solution.py:495
  34.6 0.7 copy-start.9
  35.3 14.4 %collective-permute-start.6 = (bf16[4,64,512]{2,1,0:T(8,128)(2,1)}, bf16[4,64,512]{2,1,0:T(8,128)(2,1)}, u32[]{:S(2)}, u32[]{:S(2)}) collective-permute-start(bf16[4,64,512]{2,1,0:T(8,128)(2,1)} %get-tuple-element.65), channel_id=1, source_target_pairs={{0,112},{16,0},{32,16},{48,32},{64,48},{80,64},{96,80},{112,96},{1... | collective-permute-start | bytes 786440 | tf_op jit(solution)/shard_map/ppermute | solution.py:495
  40.0 1.0 copy-start.4
  79.4 1.2 copy-start.2
  80.6 0.9 copy-start.6
  81.5 0.9 copy-start.8
  82.5 0.9 copy-start.10
  83.4 14.4 %copy-start.12 = (s32[8]{0:T(128)S(1)}, s32[8]{0:T(128)}, u32[]{:S(2)}) copy-start(s32[8]{0:T(128)} %sizes_ref.1) | copy-start | bytes 100
  83.4 15.1 %copy-start.24 = (s32[32]{0:T(128)S(1)}, s32[32]{0:T(128)}, u32[]{:S(2)}) copy-start(s32[32]{0:T(128)} %param.19) | copy-start | bytes 388
  93.2 23.7 %all-to-all-start.8 = ((bf16[128,8,512]{2,1,0:T(8,128)(2,1)}), bf16[128,8,512]{2,1,0:T(8,128)(2,1)S(1)}, u32[]{:S(2)}, u32[]{:S(2)}) async-start(bf16[128,8,512]{2,1,0:T(8,128)(2,1)} %bitcast.54), calls=%async_computation.8 | async-start | bytes 2097152 | tf_op jit(solution)/shard_map/all_to_all | solution.py:544
  97.9 38.6 %copy-start.18 = (f32[27,2048]{1,0:T(8,128)S(1)}, f32[27,2048]{1,0:T(8,128)}, u32[]{:S(2)}) copy-start(f32[27,2048]{1,0:T(8,128)} %stencil_ref.1) | copy-start | bytes 663556
  97.9 38.6 %copy-start.21 = (s32[3,2048]{1,0:T(4,128)S(1)}, s32[3,2048]{1,0:T(4,128)}, u32[]{:S(2)}) copy-start(s32[3,2048]{1,0:T(4,128)} %corner_ref.1) | copy-start | bytes 73732
  97.9 38.6 %copy-start.23 = (bf16[2048]{0:T(1024)(128)(2,1)S(1)}, bf16[2048]{0:T(1024)(128)(2,1)}, u32[]{:S(2)}) copy-start(bf16[2048]{0:T(1024)(128)(2,1)} %param.15) | copy-start | bytes 12292
  98.7 2.8 %collective-permute-start.7 = (bf16[128,256]{1,0:T(8,128)(2,1)S(1)}, bf16[128,256]{1,0:T(8,128)(2,1)S(1)}, u32[]{:S(2)}, u32[]{:S(2)}) collective-permute-start(bf16[128,256]{1,0:T(8,128)(2,1)S(1)} %maximum_bitcast_fusion.2), channel_id=1, source_target_pairs={{0,16},{16,32},{32,48},{48,64},{64,80},{80,96},{96,112},{1,17},{17... | collective-permute-start | bytes 196616 | tf_op jit(solution)/shard_map/ppermute | solution.py:574
  100.0 4.3 %collective-permute-start.8 = (bf16[128,256]{1,0:T(8,128)(2,1)S(1)}, bf16[128,256]{1,0:T(8,128)(2,1)S(1)}, u32[]{:S(2)}, u32[]{:S(2)}) collective-permute-start(bf16[128,256]{1,0:T(8,128)(2,1)S(1)} %maximum_bitcast_fusion.2), channel_id=1, source_target_pairs={{16,0},{32,16},{48,32},{64,48},{80,64},{96,80},{112,96},{17,1},{33... | collective-permute-start | bytes 196616 | tf_op jit(solution)/shard_map/ppermute | solution.py:575
  116.9 1.0 copy-start.3
  122.5 13.2 %all-to-all-start.9 = ((f32[16,1,384]{2,1,0:T(1,128)}), f32[16,1,384]{2,1,0:T(1,128)S(1)}, u32[]{:S(2)}, u32[]{:S(2)}) async-start(f32[16,1,384]{2,1,0:T(1,128)} %copy.144), calls=%async_computation.9 | async-start | bytes 49152 | tf_op jit(solution)/shard_map/all_to_all | solution.py:556
  136.4 0.7 copy-start.22

commit v3 on v2

--- a/solution.py
+++ b/solution.py
@@ -327,20 +327,20 @@
             in_ref[h] = recv_ref[:, h * 128 : h * 128 + 128].astype(f32)
 
     for s, ref in enumerate((g0_ref, g1_ref, g2_ref, g3_ref, g4_ref, g5_ref, g6_ref, g7_ref)):
-        for i in range(2):
+        for i in range(4):
             green_ref[i, (slab_ref[0] + 8 - s) % 8] = ref[i]
 
     def piece(i, xp):
         return jnp.concatenate(
             [
-                in_ref[2 * xp + h, pl.ds(4 * j + 2 * i + c, DEVS, stride=8), :].astype(bf16)
+                in_ref[2 * xp + h, pl.ds(8 * j + 2 * i + c, DEVS, stride=8), :].astype(bf16)
                 for c in range(2)
                 for h in range(2)
             ],
             axis=1,
         )
 
-    both = [jnp.concatenate([piece(i, 0), piece(i, 1)], axis=0) for i in range(2)]
+    both = [jnp.concatenate([piece(i, 0), piece(i, 1)], axis=0) for i in range(4)]
     both = [
         lax.dot_general(along_y_ref[...], t, NT, preferred_element_type=f32).astype(bf16)
         for t in both
@@ -353,7 +353,7 @@
         )
         for t in both
     ]
-    greens = [green_ref[i].reshape(L, L).astype(f32) for i in range(2)]
+    greens = [green_ref[i].reshape(L, L).astype(f32) for i in range(4)]
     both = [
         jnp.concatenate([(t[:, :L] * g).astype(bf16), (t[:, L:] * g).astype(bf16)], axis=0)
         for t, g in zip(both, greens)
@@ -370,16 +370,16 @@
         )
         for t in both
     ]
-    for i in range(2):
+    for i in range(4):
         for c in range(2):
             for xp in range(2):
                 row = c * M + xp * DEVS
                 for h in range(2):
-                    sum_ref[2 * xp + h, pl.ds(4 * j + 2 * i + c, DEVS, stride=8), :] = both[i][
+                    sum_ref[2 * xp + h, pl.ds(8 * j + 2 * i + c, DEVS, stride=8), :] = both[i][
                         row : row + DEVS, h * 128 : h * 128 + 128
                     ]
 
-    @pl.when(j == 1)
+    @pl.when(j == 0)
     def _():
         for h in range(4):
             out_ref[:, h * 128 : h * 128 + 128] = sum_ref[h].astype(bf16)
@@ -519,13 +519,13 @@
     )
     section = pl.pallas_call(
         convolve_kernel,
-        grid=(2,),
+        grid=(1,),
         out_shape=struct((2 * L, 2 * M), bf16),
         in_specs=[
             SMEM,
             pl.BlockSpec((2 * L, 2 * M), lambda j: (0, 0)),
         ]
-        + [pl.BlockSpec((2, L // 8, L), lambda j: (j, 0, 0))] * 8
+        + [pl.BlockSpec((4, L // 8, L), lambda j: (j, 0, 0))] * 8
         + [
             pl.BlockSpec((2 * L, 2 * M), lambda j: (0, 0)),
             pl.BlockSpec((2 * M, 2 * L), lambda j: (0, 0)),
@@ -536,7 +536,7 @@
         scratch_shapes=[
             pltpu.VMEM((4, 2 * L, 128), f32),
             pltpu.VMEM((4, 2 * L, 128), f32),
-            pltpu.VMEM((2, 8, L // 8, L), bf16),
+            pltpu.VMEM((4, 8, L // 8, L), bf16),
         ],
         compiler_params=LIMIT,
         name="convolve",

time: 139 us -> 140 us (level)
  Pallas kernels: 30.5 us -> 32.6 us
  transfers between devices with their start and end apart: 12 -> 12, of which waited for: 9 -> 8; matrix products, arithmetic and copies ran while one was open for 4% -> 4% of each run, Pallas kernels for 6% -> 7%
where the time goes in v3:
time: 140 us; the launch traced here: 139 us
  starting transfers between devices  34.9 us (25%)
  Pallas kernels  32.6 us (23%)
  blocking collectives  29.7 us (21%)
  waiting for transfers between devices  23.2 us (17%)
  local copies, waits for them, and re-layouts  13.4 us (10%)
  matrix products  3.36 us (2%)
  other arithmetic  1.48 us (1%)
    all_to_all x1, blocking collectives, far_field_blocks(): lax.all_to_all(section.reshape(DEVS, 8, 2 * M), ('clus', 'pen'), 0, 0, ti...  29.7 us
    ppermute x7, starting transfers between devices, far_field_blocks(): lax.ppermute(pieces[s], 'clus', [(a, (a + s) % 8) for a in range(8)])  14 us
    all_to_all x1, waiting for transfers between devices, far_field_blocks(): lax.all_to_all(section.reshape(DEVS, 8, 2 * M), ('clus', 'pen'), 0, 0, ti...  12 us
    unnamed x38, local copies, waits for them, and re-layouts  9.64 us
    pallas_call x1, Pallas kernels, far_field_blocks(): pl.pallas_call(convolve_kernel, grid=(1,), out_shape=struct((2 * L, 2 * M...  9.51 us
    all_to_all x1, starting transfers between devices, far_field_blocks(): recv = lax.all_to_all(sent, 'pen', 0, 0, tiled=True)  8.09 us
    pallas_call x1, Pallas kernels, far_field_blocks(): pl.pallas_call(bucket_kernel, out_shape=[struct((PENS, ROWS, SLOTS), bf16...  7.23 us
    ppermute x7, waiting for transfers between devices, far_field_blocks(): lax.ppermute(pieces[s], 'clus', [(a, (a + s) % 8) for a in range(8)])  5.86 us
  transfers between devices with their start and end apart: 12, of which 8 were waited for; matrix products, arithmetic and copies ran while one was open for 4% of the time, Pallas kernels for 7%

profile of v3, /device:TPU:0, one launch (start us, length us, event | category | flops | bytes accessed | tf_op | source)
XLA Modules:
  0.0 139.5 jit_solution(15735754172342165173)
XLA Ops:
  0.0 0.7 reshape.517.charge_ref
  0.7 0.7 copy-done.11
  1.4 7.2 %bucket.1 = (bf16[16,48,384]{2,1,0:T(8,128)(2,1)}, s32[8,2048]{1,0:T(8,128)S(1)}) custom-call(s32[1]{0:T(128)} %bitcast.51.slab_ref, s32[8]{0:T(128)S(1)} %copy-done.11, bf16[8,256]{1,0:T(8,128)(2,1)S(1)} %reshape.517.charge_ref, f32[27,2048]{1,0:T(8,128)} %stencil_ref.1, s32[3,2048]{1,0:T(4,128)} %corner_ref.1), custom_call_target="tpu_custom_call" | custom-call | tf_op jit(solution)/shard_map/bucket/pallas_call | solution.py:461
  8.6 8.1 %all-to-all-start.6 = ((bf16[16,48,384]{2,1,0:T(8,128)(2,1)}), bf16[16,48,384]{2,1,0:T(8,128)(2,1)S(1)}, u32[]{:S(2)}, u32[]{:S(2)}) async-start(bf16[16,48,384]{2,1,0:T(8,128)(2,1)} %get-tuple-element.54), calls=%async_computation.6 | async-start | bytes 1179648 | tf_op jit(solution)/shard_map/all_to_all | solution.py:493
  16.7 5.4 %recut.1 = (bf16[4,64,512]{2,1,0:T(8,128)(2,1)S(1)}, bf16[4,64,512]{2,1,0:T(8,128)(2,1)S(1)}, bf16[4,64,512]{2,1,0:T(8,128)(2,1)S(1)}, bf16[4,64,512]{2,1,0:T(8,...) custom-call(s32[1]{0:T(128)} %bitcast.51.slab_ref, ...), custom_call_target="tpu_custom_call" | custom-call | tf_op jit(solution)/shard_map/recut/pallas_call | solution.py:484
  22.1 0.7 copy-done.5
  22.8 0.0 collective-permute-start
  22.8 1.6 %collective-permute-start.1 = (bf16[4,64,512]{2,1,0:T(8,128)(2,1)S(1)}, bf16[4,64,512]{2,1,0:T(8,128)(2,1)S(1)}, u32[]{:S(2)}, u32[]{:S(2)}) collective-permute-start(bf16[4,64,512]{2,1,0:T(8,128)(2,1)S(1)} %get-tuple-element.60), channel_id=1, source_target_pairs={{0,32},{16,48},{32,64},{48,80},{64,96},{80,112},{96,0},{112,16},{1... | collective-permute-start | bytes 786440 | tf_op jit(solution)/shard_map/ppermute | solution.py:495
  24.4 2.3 %collective-permute-start.2 = (bf16[4,64,512]{2,1,0:T(8,128)(2,1)}, bf16[4,64,512]{2,1,0:T(8,128)(2,1)}, u32[]{:S(2)}, u32[]{:S(2)}) collective-permute-start(bf16[4,64,512]{2,1,0:T(8,128)(2,1)} %get-tuple-element.61), channel_id=1, source_target_pairs={{0,48},{16,64},{32,80},{48,96},{64,112},{80,0},{96,16},{112,32},{1... | collective-permute-start | bytes 786440 | tf_op jit(solution)/shard_map/ppermute | solution.py:495
  26.6 1.8 %collective-permute-start.3 = (bf16[4,64,512]{2,1,0:T(8,128)(2,1)}, bf16[4,64,512]{2,1,0:T(8,128)(2,1)}, u32[]{:S(2)}, u32[]{:S(2)}) collective-permute-start(bf16[4,64,512]{2,1,0:T(8,128)(2,1)} %get-tuple-element.62), channel_id=1, source_target_pairs={{0,64},{16,80},{32,96},{48,112},{64,0},{80,16},{96,32},{112,48},{1... | collective-permute-start | bytes 786440 | tf_op jit(solution)/shard_map/ppermute | solution.py:495
  28.5 1.8 %collective-permute-start.4 = (bf16[4,64,512]{2,1,0:T(8,128)(2,1)}, bf16[4,64,512]{2,1,0:T(8,128)(2,1)}, u32[]{:S(2)}, u32[]{:S(2)}) collective-permute-start(bf16[4,64,512]{2,1,0:T(8,128)(2,1)} %get-tuple-element.63), channel_id=1, source_target_pairs={{0,80},{16,96},{32,112},{48,0},{64,16},{80,32},{96,48},{112,64},{1... | collective-permute-start | bytes 786440 | tf_op jit(solution)/shard_map/ppermute | solution.py:495
  30.3 1.8 %collective-permute-done.g1_ref = bf16[4,64,512]{2,1,0:T(8,128)(2,1)S(1)} collective-permute-done((bf16[4,64,512]{2,1,0:T(8,128)(2,1)S(1)}, bf16[4,64,512]{2,1,0:T(8,128)(2,1)S(1)}, u32[]{:S(2)}, u32[]{:S(2)}) %collective-permute-start) | collective-permute-done | bytes 262176 | tf_op jit(solution)/shard_map/ppermute | solution.py:495
  32.0 0.7 copy-done.7
  32.7 1.8 %collective-permute-start.5 = (bf16[4,64,512]{2,1,0:T(8,128)(2,1)}, bf16[4,64,512]{2,1,0:T(8,128)(2,1)}, u32[]{:S(2)}, u32[]{:S(2)}) collective-permute-start(bf16[4,64,512]{2,1,0:T(8,128)(2,1)} %get-tuple-element.64), channel_id=1, source_target_pairs={{0,96},{16,112},{32,0},{48,16},{64,32},{80,48},{96,64},{112,80},{1... | collective-permute-start | bytes 786440 | tf_op jit(solution)/shard_map/ppermute | solution.py:495
  34.6 0.0 collective-permute-done.1.g2_ref
  34.6 0.7 copy-done.9
  35.3 4.7 %collective-permute-start.6 = (bf16[4,64,512]{2,1,0:T(8,128)(2,1)}, bf16[4,64,512]{2,1,0:T(8,128)(2,1)}, u32[]{:S(2)}, u32[]{:S(2)}) collective-permute-start(bf16[4,64,512]{2,1,0:T(8,128)(2,1)} %get-tuple-element.65), channel_id=1, source_target_pairs={{0,112},{16,0},{32,16},{48,32},{64,48},{80,64},{96,80},{112,96},{1... | collective-permute-start | bytes 786440 | tf_op jit(solution)/shard_map/ppermute | solution.py:495
  40.0 0.0 all-to-all-done.6.recv_ref
  40.0 1.0 copy-done.4
  41.0 4.5 %deposit.1 = (bf16[1024,512]{1,0:T(8,128)(2,1)S(1)}, f32[24,6656]{1,0:T(8,128)S(1)}, s32[17]{0:T(128)S(1)}) custom-call(bf16[16,48,384]{2,1,0:T(8,128)(2,1)S(1)} %all-to-all-done.6.recv_ref, bf16[1024,256]{1,0:T(8,128)(2,1)S(1)} %copy-done.4), custom_call_target="tpu_custom_call" | custom-call | tf_op jit(solution)/shard_map/deposit/pallas_call | solution.py:498
  45.6 0.0 collective-permute-done.2.g3_ref
  45.6 0.1 collective-permute-done.3.g4_ref
  45.7 1.8 %collective-permute-done.4.g5_ref = bf16[4,64,512]{2,1,0:T(8,128)(2,1)} collective-permute-done((bf16[4,64,512]{2,1,0:T(8,128)(2,1)}, bf16[4,64,512]{2,1,0:T(8,128)(2,1)}, u32[]{:S(2)}, u32[]{:S(2)}) %collective-permute-start.4) | collective-permute-done | bytes 262176 | tf_op jit(solution)/shard_map/ppermute | solution.py:495
  47.5 0.4 collective-permute-done.5.g6_ref
  47.9 1.7 %collective-permute-done.6.g7_ref = bf16[4,64,512]{2,1,0:T(8,128)(2,1)} collective-permute-done((bf16[4,64,512]{2,1,0:T(8,128)(2,1)}, bf16[4,64,512]{2,1,0:T(8,128)(2,1)}, u32[]{:S(2)}, u32[]{:S(2)}) %collective-permute-start.6) | collective-permute-done | bytes 262176 | tf_op jit(solution)/shard_map/ppermute | solution.py:495
  49.7 29.7 %all_to_all.68 = bf16[128,8,512]{2,1,0:T(8,128)(2,1)S(1)} all-to-all(bf16[128,8,512]{2,1,0:T(8,128)(2,1)S(1)} %bitcast.149), channel_id=1, replica_groups=mesh['clus'=8,'pen'=16] {'clus','pen'}, dimensions={0} | all-to-all | bytes 2097152 | tf_op jit(solution)/shard_map/all_to_all | solution.py:517
  79.4 0.0 copy-done
  79.4 0.0 copy-done.1
  79.4 1.2 copy-done.2
  80.6 0.9 copy-done.6
  81.5 0.9 copy-done.8
  82.5 0.9 copy-done.10
  83.4 9.5 %convolve.1 = bf16[1024,512]{1,0:T(8,128)(2,1)} custom-call(s32[1]{0:T(128)} %bitcast.51.slab_ref, bf16[1024,512]{1,0:T(8,128)(2,1)S(1)} %bitcast.147, bf16[4,64,512]{2,1,0:T(8,128)(2,1)S(1)} %copy-done.6, bf16[4,64,512]{2,1,0:T(8,128)(2,1)S(1)} %copy-done.8, bf16[4,64,512]{2,1,0:T(8,128)(2,1)S(1)} %copy-done.10, ...), custom_call_target="tpu_custom_call" | custom-call | tf_op jit(solution)/shard_map/convolve/pallas_call | solution.py:520
  92.9 4.6 %all-to-all-start.8 = ((bf16[128,8,512]{2,1,0:T(8,128)(2,1)}), bf16[128,8,512]{2,1,0:T(8,128)(2,1)S(1)}, u32[]{:S(2)}, u32[]{:S(2)}) async-start(bf16[128,8,512]{2,1,0:T(8,128)(2,1)} %bitcast.54), calls=%async_computation.8 | async-start | bytes 2097152 | tf_op jit(solution)/shard_map/all_to_all | solution.py:544
  97.6 0.0 copy-done.12
  97.6 0.0 copy-start.18
  97.6 0.0 copy-start.21
  97.6 0.0 copy-start.23
  97.6 0.1 iota_compare_fusion
  97.7 0.6 lt.82
  98.3 0.0 copy-done.24
  98.4 1.3 collective-permute-start.7
  99.7 1.3 collective-permute-start.8
  101.0 0.0 collective-permute-done.7
  101.1 2.9 %collective-permute-done.8 = bf16[128,256]{1,0:T(8,128)(2,1)S(1)} collective-permute-done((bf16[128,256]{1,0:T(8,128)(2,1)S(1)}, bf16[128,256]{1,0:T(8,128)(2,1)S(1)}, u32[]{:S(2)}, u32[]{:S(2)}) %collective-permute-start.8) | collective-permute-done | bytes 65568 | tf_op jit(solution)/shard_map/ppermute | solution.py:575
  104.0 0.6 gather_fusion.1
  104.6 12.0 %all-to-all-done.8 = bf16[128,8,512]{2,1,0:T(8,128)(2,1)S(1)} async-done(((bf16[128,8,512]{2,1,0:T(8,128)(2,1)}), bf16[128,8,512]{2,1,0:T(8,128)(2,1)S(1)}, u32[]{:S(2)}, u32[]{:S(2)}) %all-to-all-start.8) | async-done | bytes 1048608 | tf_op jit(solution)/shard_map/all_to_all | solution.py:544
  116.6 1.0 copy-done.3
  117.7 5.2 %interpolate.1 = (f32[16,384]{1,0:T(8,128)S(1)}, f32[8,128]{1,0:T(8,128)S(1)}) custom-call(s32[17]{0:T(128)S(1)} %get-tuple-element.55.meta_ref, bf16[1024,512]{1,0:T(8,128)(2,1)S(1)} %bitcast.148, bf16[256,1024]{1,0:T(8,128)(2,1)S(1)} %copy-done.3, f32[24,6656]{1,0:T(8,128)S(1)} %get-tuple-element.75.packed_ref), custom_call_target="tpu_custom_call" | custom-call | tf_op jit(solution)/shard_map/interpolate/pallas_call | solution.py:547
  122.9 0.6 copy.144
  123.5 5.6 %all-to-all-start.9 = ((f32[16,1,384]{2,1,0:T(1,128)}), f32[16,1,384]{2,1,0:T(1,128)S(1)}, u32[]{:S(2)}, u32[]{:S(2)}) async-start(f32[16,1,384]{2,1,0:T(1,128)} %copy.144), calls=%async_computation.9 | async-start | bytes 49152 | tf_op jit(solution)/shard_map/all_to_all | solution.py:556
  129.2 3.4 %fusion.42 = f32[32,1,256]{2,1,0:T(1,128)S(1)} fusion(bf16[32,256,256]{2,1,0:T(8,128)(2,1)} %param.20, bf16[32,256,1]{1,0,2:T(8,128)(2,1)S(1)} %bitcast.170), kind=kOutput, calls=%fused_computation.78 | convolution fusion | flops 4194304 | bytes 4243456 | tf_op jit(solution)/shard_map/pjm,pm->pj/dot_general | solution.py:589
  132.6 0.6 copy.167
  133.2 0.5 slice.25
  134.4 2.4 %all-to-all-done.9 = f32[16,1,384]{2,1,0:T(1,128)S(1)} async-done(((f32[16,1,384]{2,1,0:T(1,128)}), f32[16,1,384]{2,1,0:T(1,128)S(1)}, u32[]{:S(2)}, u32[]{:S(2)}) %all-to-all-start.9) | async-done | bytes 24608 | tf_op jit(solution)/shard_map/all_to_all | solution.py:556
  136.8 0.7 collect.1
  137.4 0.0 copy-done.18
  137.5 0.0 copy-done.21
  137.5 0.0 copy-done.23
  137.5 0.0 copy-start.22
  137.5 0.6 conditional.1
  137.5 0.6 slice.17
  138.1 0.1 copy-done.22
  138.2 1.3 add_select_fusion.1
  (25 shorter events, 0.2 us)
Async XLA Ops:
  0.7 0.7 copy-start.11
  8.6 70.8 %copy-start = (bf16[512,1024]{1,0:T(8,128)(2,1)S(1)}, bf16[512,1024]{1,0:T(8,128)(2,1)}, u32[]{:S(2)}) copy-start(bf16[512,1024]{1,0:T(8,128)(2,1)} %constant.104.clone.along_x_ref.back_x_ref) | copy-start | bytes 3145732
  8.6 70.8 %copy-start.1 = (bf16[1024,512]{1,0:T(8,128)(2,1)S(1)}, bf16[1024,512]{1,0:T(8,128)(2,1)}, u32[]{:S(2)}) copy-start(bf16[1024,512]{1,0:T(8,128)(2,1)} %constant.103.clone.along_y_ref) | copy-start | bytes 3145732
  8.6 31.4 %all-to-all-start.6 = ((bf16[16,48,384]{2,1,0:T(8,128)(2,1)}), bf16[16,48,384]{2,1,0:T(8,128)(2,1)S(1)}, u32[]{:S(2)}, u32[]{:S(2)}) async-start(bf16[16,48,384]{2,1,0:T(8,128)(2,1)} %get-tuple-element.54), calls=%async_computation.6 | async-start | bytes 1179648 | tf_op jit(solution)/shard_map/all_to_all | solution.py:493
  22.1 0.7 copy-start.5
  22.8 9.3 %collective-permute-start = (bf16[4,64,512]{2,1,0:T(8,128)(2,1)S(1)}, bf16[4,64,512]{2,1,0:T(8,128)(2,1)S(1)}, u32[]{:S(2)}, u32[]{:S(2)}) collective-permute-start(bf16[4,64,512]{2,1,0:T(8,128)(2,1)S(1)} %get-tuple-element.59), channel_id=1, source_target_pairs={{0,16},{16,32},{32,48},{48,64},{64,80},{80,96},{96,112},{112,0},{1... | collective-permute-start | bytes 786440 | tf_op jit(solution)/shard_map/ppermute | solution.py:495
  22.8 11.8 %collective-permute-start.1 = (bf16[4,64,512]{2,1,0:T(8,128)(2,1)S(1)}, bf16[4,64,512]{2,1,0:T(8,128)(2,1)S(1)}, u32[]{:S(2)}, u32[]{:S(2)}) collective-permute-start(bf16[4,64,512]{2,1,0:T(8,128)(2,1)S(1)} %get-tuple-element.60), channel_id=1, source_target_pairs={{0,32},{16,48},{32,64},{48,80},{64,96},{80,112},{96,0},{112,16},{1... | collective-permute-start | bytes 786440 | tf_op jit(solution)/shard_map/ppermute | solution.py:495
  24.4 21.2 %collective-permute-start.2 = (bf16[4,64,512]{2,1,0:T(8,128)(2,1)}, bf16[4,64,512]{2,1,0:T(8,128)(2,1)}, u32[]{:S(2)}, u32[]{:S(2)}) collective-permute-start(bf16[4,64,512]{2,1,0:T(8,128)(2,1)} %get-tuple-element.61), channel_id=1, source_target_pairs={{0,48},{16,64},{32,80},{48,96},{64,112},{80,0},{96,16},{112,32},{1... | collective-permute-start | bytes 786440 | tf_op jit(solution)/shard_map/ppermute | solution.py:495
  26.6 19.1 %collective-permute-start.3 = (bf16[4,64,512]{2,1,0:T(8,128)(2,1)}, bf16[4,64,512]{2,1,0:T(8,128)(2,1)}, u32[]{:S(2)}, u32[]{:S(2)}) collective-permute-start(bf16[4,64,512]{2,1,0:T(8,128)(2,1)} %get-tuple-element.62), channel_id=1, source_target_pairs={{0,64},{16,80},{32,96},{48,112},{64,0},{80,16},{96,32},{112,48},{1... | collective-permute-start | bytes 786440 | tf_op jit(solution)/shard_map/ppermute | solution.py:495
  28.5 19.0 %collective-permute-start.4 = (bf16[4,64,512]{2,1,0:T(8,128)(2,1)}, bf16[4,64,512]{2,1,0:T(8,128)(2,1)}, u32[]{:S(2)}, u32[]{:S(2)}) collective-permute-start(bf16[4,64,512]{2,1,0:T(8,128)(2,1)} %get-tuple-element.63), channel_id=1, source_target_pairs={{0,80},{16,96},{32,112},{48,0},{64,16},{80,32},{96,48},{112,64},{1... | collective-permute-start | bytes 786440 | tf_op jit(solution)/shard_map/ppermute | solution.py:495
  32.0 0.7 copy-start.7
  32.7 15.2 %collective-permute-start.5 = (bf16[4,64,512]{2,1,0:T(8,128)(2,1)}, bf16[4,64,512]{2,1,0:T(8,128)(2,1)}, u32[]{:S(2)}, u32[]{:S(2)}) collective-permute-start(bf16[4,64,512]{2,1,0:T(8,128)(2,1)} %get-tuple-element.64), channel_id=1, source_target_pairs={{0,96},{16,112},{32,0},{48,16},{64,32},{80,48},{96,64},{112,80},{1... | collective-permute-start | bytes 786440 | tf_op jit(solution)/shard_map/ppermute | solution.py:495
  34.6 0.7 copy-start.9
  35.3 14.4 %collective-permute-start.6 = (bf16[4,64,512]{2,1,0:T(8,128)(2,1)}, bf16[4,64,512]{2,1,0:T(8,128)(2,1)}, u32[]{:S(2)}, u32[]{:S(2)}) collective-permute-start(bf16[4,64,512]{2,1,0:T(8,128)(2,1)} %get-tuple-element.65), channel_id=1, source_target_pairs={{0,112},{16,0},{32,16},{48,32},{64,48},{80,64},{96,80},{112,96},{1... | collective-permute-start | bytes 786440 | tf_op jit(solution)/shard_map/ppermute | solution.py:495
  40.0 1.0 copy-start.4
  79.4 1.2 copy-start.2
  80.6 0.9 copy-start.6
  81.5 0.9 copy-start.8
  82.5 0.9 copy-start.10
  83.4 14.2 %copy-start.12 = (s32[8]{0:T(128)S(1)}, s32[8]{0:T(128)}, u32[]{:S(2)}) copy-start(s32[8]{0:T(128)} %sizes_ref.1) | copy-start | bytes 100
  83.4 14.9 %copy-start.24 = (s32[32]{0:T(128)S(1)}, s32[32]{0:T(128)}, u32[]{:S(2)}) copy-start(s32[32]{0:T(128)} %param.19) | copy-start | bytes 388
  92.9 23.7 %all-to-all-start.8 = ((bf16[128,8,512]{2,1,0:T(8,128)(2,1)}), bf16[128,8,512]{2,1,0:T(8,128)(2,1)S(1)}, u32[]{:S(2)}, u32[]{:S(2)}) async-start(bf16[128,8,512]{2,1,0:T(8,128)(2,1)} %bitcast.54), calls=%async_computation.8 | async-start | bytes 2097152 | tf_op jit(solution)/shard_map/all_to_all | solution.py:544
  97.6 39.9 %copy-start.18 = (f32[27,2048]{1,0:T(8,128)S(1)}, f32[27,2048]{1,0:T(8,128)}, u32[]{:S(2)}) copy-start(f32[27,2048]{1,0:T(8,128)} %stencil_ref.1) | copy-start | bytes 663556
  97.6 39.9 %copy-start.21 = (s32[3,2048]{1,0:T(4,128)S(1)}, s32[3,2048]{1,0:T(4,128)}, u32[]{:S(2)}) copy-start(s32[3,2048]{1,0:T(4,128)} %corner_ref.1) | copy-start | bytes 73732
  97.6 39.8 %copy-start.23 = (bf16[2048]{0:T(1024)(128)(2,1)S(1)}, bf16[2048]{0:T(1024)(128)(2,1)}, u32[]{:S(2)}) copy-start(bf16[2048]{0:T(1024)(128)(2,1)} %param.15) | copy-start | bytes 12292
  98.4 2.6 %collective-permute-start.7 = (bf16[128,256]{1,0:T(8,128)(2,1)S(1)}, bf16[128,256]{1,0:T(8,128)(2,1)S(1)}, u32[]{:S(2)}, u32[]{:S(2)}) collective-permute-start(bf16[128,256]{1,0:T(8,128)(2,1)S(1)} %maximum_bitcast_fusion.2), channel_id=1, source_target_pairs={{0,16},{16,32},{32,48},{48,64},{64,80},{80,96},{96,112},{1,17},{17... | collective-permute-start | bytes 196616 | tf_op jit(solution)/shard_map/ppermute | solution.py:574
  99.7 4.3 %collective-permute-start.8 = (bf16[128,256]{1,0:T(8,128)(2,1)S(1)}, bf16[128,256]{1,0:T(8,128)(2,1)S(1)}, u32[]{:S(2)}, u32[]{:S(2)}) collective-permute-start(bf16[128,256]{1,0:T(8,128)(2,1)S(1)} %maximum_bitcast_fusion.2), channel_id=1, source_target_pairs={{16,0},{32,16},{48,32},{64,48},{80,64},{96,80},{112,96},{17,1},{33... | collective-permute-start | bytes 196616 | tf_op jit(solution)/shard_map/ppermute | solution.py:575
  116.6 1.0 copy-start.3
  123.5 13.2 %all-to-all-start.9 = ((f32[16,1,384]{2,1,0:T(1,128)}), f32[16,1,384]{2,1,0:T(1,128)S(1)}, u32[]{:S(2)}, u32[]{:S(2)}) async-start(f32[16,1,384]{2,1,0:T(1,128)} %copy.144), calls=%async_computation.9 | async-start | bytes 49152 | tf_op jit(solution)/shard_map/all_to_all | solution.py:556
  137.5 0.7 copy-start.22
